TPU v7x, 32 devices: a whole 2x2x4 slice. The times are simulated.
32 devices in a mesh: col: 8 (over z, x), rep: 4 (over y, core).
Axes of the slice: x: 2, y: 2, z: 4, core: 2. Of those that a mesh axis runs over, the one named last changes fastest.
Arguments:
- coords: bfloat16 [65536, 128], P(('col', 'rep')), may hold values from -6 to 6
- dissim: bfloat16 [32, 5, 64, 128, 128], P(('col', 'rep')), may hold values from 8 to 24
- tile_blocks: int32 [32, 5, 64, 2], P(('col', 'rep')), may hold values from 0 to 63, as said below
- tile_count: int32 [32, 5], P(('col', 'rep')), may hold values from 8 to 64, as said below
Outputs:
- updated: float32 [65536, 128], P(('col', 'rep'))
Inputs may be any that keep to these rules, and one draw needn't show every extreme that they name: `tile_blocks`: within one list and offset no (row block, column block) pair repeats; slots at or past the live count are ignored. `tile_count`: A list has equally many live slots at every offset; some list has 64 at every offset.
All inputs are finite; a program needn't handle non-finite values.
Results may differ from a plain program's by a relative error of at most 0.0003.
Values may be sent and summed in bfloat16 or wider, within the bound.
No kernel may reach another device: no remote copies, remote signals or barrier semaphores. Data moves between devices by JAX's collectives and lax.ppermute only.
A program may use at most 128 MiB of HBM per device.

v0:
```python
import functools

import jax
import jax.numpy as jnp
from jax import lax
from jax.experimental import pallas as pl
from jax.experimental.pallas import tpu as pltpu
from jax.sharding import PartitionSpec as P

GROUP = 16
SUM_GROUP = 8
COST = 0.25
VMEM_LIMIT = 34 * 1024 * 1024
VMEM, SMEM, HBM = pltpu.VMEM, pltpu.SMEM, pltpu.HBM
STAGES = (
    ((0, 0), (1, 1), (4, 4)),
    ((2, 2), (5, 5), (8, 8)),
    ((9, 9), (3, 7), (6, 6)),
    ((7, 3),),
)


def place_of_device(stride):
    return lax.axis_index("rep"), lax.rem(lax.div(lax.axis_index("col"), stride), 2) == 0


def lanes_of(shape):
    return lax.broadcasted_iota(jnp.int32, shape, len(shape) - 1)


def diagonal(side):
    return lax.broadcasted_iota(jnp.int32, (side, side), 0) == lanes_of((side, side))


def row_of(column):
    return jnp.sum(jnp.where(diagonal(column.shape[0]), column, 0.0), axis=0, keepdims=True)


def column_of(row):
    return jnp.sum(jnp.where(diagonal(row.shape[1]), row, 0.0), axis=1, keepdims=True)


def lists_kernel(stride, per_quarter, codes, out):
    rep, even = place_of_device(stride)
    core, mine = rep & 1, lax.shift_right_arithmetic(rep, 1)
    offsets, width = codes.shape
    room = out.shape[1] - 128
    lanes = lanes_of((1, width))
    later = lax.broadcasted_iota(jnp.int32, (width, width), 0) <= lanes_of((width, width))
    later = jnp.where(later, 1.0, 0.0).astype(jnp.bfloat16)
    place_of = lax.broadcasted_iota(jnp.int32, (room, width), 0).astype(jnp.float32) + 1.0
    for stage, arrays in enumerate(STAGES):
        before = jnp.zeros((1, 1), jnp.float32)
        listed = jnp.zeros((32, room), jnp.float32)
        for offset in range(offsets):
            here = [(m, *pair) for m, pair in enumerate(arrays) if offset in (pair[0] // 2, pair[1] // 2)]
            if not here:
                continue
            code = codes[offset : offset + 1, :]
            row, col = lax.shift_right_arithmetic(code, 8), code & 255
            quarter = jnp.zeros_like(col)
            for edge in range(1, 4):
                quarter += jnp.where(col >= edge * per_quarter, 1, 0)
            match = jnp.zeros((1, width), jnp.float32)
            column = (col - quarter * per_quarter).astype(jnp.float32)
            for index, at_even, at_odd in here:
                piece = jnp.where(even, at_even, at_odd)
                wanted = jnp.bitwise_xor(mine, piece & 1) * 2 + core
                wanted = jnp.where(lax.shift_right_arithmetic(piece, 1) == offset, wanted, -1)
                hit = jnp.where((code >= 0) & (quarter == wanted), 1.0, 0.0)
                match += hit
                column += hit * (index * per_quarter)
            found = before + jnp.dot(
                jnp.broadcast_to(match, (16, width)).astype(jnp.bfloat16), later, preferred_element_type=jnp.float32
            )[0:1]
            before += jnp.sum(match, axis=1, keepdims=True)
            chosen = jnp.where((place_of == found) & (match > 0.0), 1.0, 0.0).astype(jnp.bfloat16)
            values = [lanes.astype(jnp.float32), row.astype(jnp.float32), column, jnp.full((1, width), offset, jnp.float32)]
            values = jnp.concatenate([jnp.broadcast_to(v, (8, width)) for v in values], axis=0).astype(jnp.bfloat16)
            listed += lax.dot_general(
                values, chosen, (((1,), (1,)), ((), ())), preferred_element_type=jnp.float32
            )
        listed = listed.astype(jnp.int32)
        lane, row, column, offset = listed[0:1], listed[8:9], listed[16:17], listed[24:25]
        slots = width // 2
        tile = offset * slots + lane + jnp.where(lane >= slots, (offsets - 1) * slots, 0)
        out[stage : stage + 1, :room] = tile * 65536 + row * 256 + column
        out[stage : stage + 1, room:] = jnp.broadcast_to(before.astype(jnp.int32), (1, 128))


def weights_kernel(codes, counts, targets, out, sums):
    step = pl.program_id(0)
    blocks, side = out.shape
    total = counts[step]

    @pl.when(step == 0)
    def _():
        sums[...] = jnp.zeros_like(sums)

    def visit(group, carry):
        for unit in range(SUM_GROUP):
            slot = group * SUM_GROUP + unit
            row = jnp.where(slot < total, lax.shift_right_arithmetic(codes[step, slot], 8), blocks)
            share = pltpu.reciprocal(targets[0, slot].astype(jnp.float32), approx=True)
            sums[row] += share * share
        return carry

    lax.fori_loop(0, (total + SUM_GROUP - 1) // SUM_GROUP, visit, 0)

    @pl.when(step == pl.num_programs(0) - 1)
    def _():
        def close(group, carry):
            for unit in range(8):
                whole = jnp.sum(sums[group * 8 + unit], axis=1, keepdims=True)
                out[pl.ds(group * 8 + unit, 1), :] = row_of(whole)
            return carry

        lax.fori_loop(0, blocks // 8, close, 0)


def scale_kernel(weights, more_weights, out):
    count = weights.shape[0] // 4
    side = weights.shape[1]
    own = pl.ds(pl.multiple_of(lax.axis_index("rep") * count, count), count)
    own = weights[own, :] + more_weights[own, :]
    for block in range(count):
        total = column_of(own[block : block + 1, :])
        out[block * side : (block + 1) * side, :] = jnp.broadcast_to(1.0 / (total + 1.0), (side, side))


def rows_kernel(q0, q1, q2, q3, out, norms):
    side = out.shape[1]
    count = q0.shape[0] // side
    for index, quarter in enumerate((q0, q1, q2, q3)):
        holder = jnp.bitwise_xor(lax.axis_index("rep"), index)

        def visit(block, carry, quarter=quarter, holder=holder):
            points = quarter[pl.ds(pl.multiple_of(block * side, side), side), :].astype(jnp.float32)
            out[holder * count + block] = (-2.0 * points).astype(jnp.bfloat16)
            norm = jnp.sum(points * points, axis=1, keepdims=True) + 1.0
            norms[holder * count + block] = jnp.broadcast_to(norm, (side, side))
            return carry

        lax.fori_loop(0, count, visit, 0, unroll=4)


def stage_kernel(stage, first, layout, stride, tokens, lists, rows, norms, *rest):
    parts = len(layout)
    points_refs, (own, other), rest = rest[:parts], rest[parts : parts + 2], rest[parts + 2 :]
    rest = rest[tokens:] if first else rest[tokens + 2 :]
    even = place_of_device(stride)[1]
    pulled, summed, token, right, column_norms, ring, ratios, sems = rest
    side = rows.shape[1]
    tiles = own.shape[0]
    dummy = pulled.shape[0] - 1
    total = lists[stage, lists.shape[1] - 1]
    groups = (total + GROUP - 1) // GROUP
    token[...] = jnp.zeros_like(token)

    def entry(index):
        return lists[stage, jnp.minimum(index, total - 1)]

    def fetch(group, slot):
        for unit in range(GROUP):
            tile = lax.shift_right_arithmetic(entry(group * GROUP + unit), 16)

            @pl.when(tile < tiles)
            def _():
                pltpu.make_async_copy(own.at[tile], ring.at[slot, unit], sems.at[slot]).start()

            @pl.when(tile >= tiles)
            def _():
                pltpu.make_async_copy(other.at[tile - tiles], ring.at[slot, unit], sems.at[slot]).start()

    @pl.when(groups > 0)
    def _():
        fetch(0, 0)

    if first:
        pulled[...] = jnp.zeros_like(pulled)
        summed[...] = jnp.zeros_like(summed)

    @pl.when(groups > 0)
    def _():
        for points_ref, (at, parity) in zip(points_refs, layout, strict=True):

            def build(block, carry, points_ref=points_ref, at=at):
                points = points_ref[pl.ds(pl.multiple_of(block * side, side), side), :]
                right[at + block] = points
                points = points.astype(jnp.float32)
                column_norms[pl.ds(at + block, 1), :] = row_of(jnp.sum(points * points, axis=1, keepdims=True))
                return carry

            held = points_ref.shape[0] // side // 4

            def build_four(four, carry, build=build):
                for unit in range(4):
                    build(four * 4 + unit, carry)
                return carry

            if parity is not None:
                held = jnp.where(even == (parity == 1), held, 0)
            lax.fori_loop(0, held, build_four, 0)

    def visit(group, carry):
        slot = lax.rem(group, 2)

        @pl.when(group + 1 < groups)
        def _():
            fetch(group + 1, 1 - slot)

        pltpu.make_async_copy(own.at[pl.ds(0, GROUP)], ring.at[slot], sems.at[slot]).wait()
        for unit in range(GROUP):
            code = entry(group * GROUP + unit)
            row, column = lax.shift_right_arithmetic(code, 8) & 255, code & 255
            square = lax.dot_general(
                rows[row], right[column], (((1,), (1,)), ((), ())), preferred_element_type=jnp.float32
            )
            square += norms[row] + column_norms[pl.ds(column, 1), :]
            share = pltpu.reciprocal(ring[slot, unit].astype(jnp.float32), approx=True)
            ratios[unit] = (share * (share - lax.rsqrt(square))).astype(jnp.bfloat16)
        for unit in range(GROUP):
            index = group * GROUP + unit
            code = entry(index)
            place = jnp.where(index < total, lax.shift_right_arithmetic(code, 8) & 255, dummy)
            pulled[place] += jnp.dot(ratios[unit], right[code & 255], preferred_element_type=jnp.float32)
            summed[place] += ratios[unit].astype(jnp.float32)
        return carry

    lax.fori_loop(0, groups, visit, 0)


def gate_kernel(*refs):
    pass


def halves_kernel(first, second, weights, more_weights, *rest):
    upper, lower, total = rest[-3:]
    half = upper.shape[0]
    upper[...] = first[:half, :]
    lower[...] = second[half:, :]
    total[...] = weights[...] + more_weights[...]


def choose_kernel(stride, at_even, at_odd, out):
    even = place_of_device(stride)[1]

    @pl.when(even)
    def _():
        out[...] = at_even[...]

    @pl.when(jnp.logical_not(even))
    def _():
        out[...] = at_odd[...]


def drift(pulled, summed, block, points):
    return pulled[block] - jnp.sum(summed[block], axis=1, keepdims=True) * points


def pack_core_kernel(flip, pulled, summed, points_ref, out):
    side = pulled.shape[1]
    count = (pulled.shape[0] - 1) // 4
    base = jnp.bitwise_xor(lax.axis_index("rep"), flip) * count
    for block in range(count):
        rows = slice(block * side, (block + 1) * side)
        out[rows, :] = drift(pulled, summed, base + block, points_ref[rows, :].astype(jnp.float32))


def pack_far_kernel(pulled, summed, norms, got, points_ref, out):
    side = pulled.shape[1]
    count = (pulled.shape[0] - 1) // 4
    base = jnp.bitwise_xor(lax.axis_index("rep"), 2) * count
    ones = jnp.ones((side, side), jnp.bfloat16)
    shares = []
    for block in range(count):
        rows = slice(block * side, (block + 1) * side)
        points = points_ref[rows, :].astype(jnp.float32)
        total = drift(pulled, summed, base + block, points) + got[rows, :]
        along = jnp.dot((total * points).astype(jnp.bfloat16), ones, preferred_element_type=jnp.float32)
        share = (along * pltpu.reciprocal(norms[base + block] - (1.0 - 1e-6), approx=True)).astype(jnp.bfloat16).astype(jnp.float32)
        out[rows, :] = (total - share * points).astype(jnp.bfloat16)
        shares.append(jnp.sum(jnp.where(diagonal(side), share, 0.0), axis=0, keepdims=True))
    out[count * side :, :] = jnp.concatenate(shares, axis=0).astype(jnp.bfloat16)


def base_kernel(pulled, summed, near, scale, points_ref, out):
    side = pulled.shape[1]
    count = (pulled.shape[0] - 1) // 4
    base = lax.axis_index("rep") * count
    for block in range(count):
        rows = slice(block * side, (block + 1) * side)
        points = points_ref[rows, :].astype(jnp.float32)
        total = drift(pulled, summed, base + block, points) + near[rows, :]
        out[rows, :] = points + scale[rows, :] * total


def finish_kernel(base, far, scale, points_ref, out):
    count, side = far.shape[0] - points_ref.shape[0], far.shape[1]
    shares = far[count * side :, :].astype(jnp.float32)
    for block in range(count):
        rows = slice(block * side, (block + 1) * side)
        points = points_ref[rows, :].astype(jnp.float32)
        total = far[rows, :].astype(jnp.float32) + column_of(shares[block : block + 1, :]) * points
        out[rows, :] = base[rows, :] + scale[rows, :] * total


def kernel_call(body, name, cost, **options):
    return pl.pallas_call(
        body,
        name=name,
        compiler_params=pltpu.CompilerParams(vmem_limit_bytes=VMEM_LIMIT),
        cost_estimate=pl.CostEstimate(
            flops=int(cost * COST * 1e9), bytes_accessed=int(cost * COST * 3e6), transcendentals=0
        ),
        **options,
    )


def per_device(coords, dissim, tile_blocks, tile_count):
    own_rows, width = coords.shape
    _, offsets, slots, side, _ = dissim.shape
    targets = dissim.reshape(offsets * slots, side, side)
    reps = lax.axis_size("rep")
    stride = lax.axis_size("col") // 8
    count = own_rows // side
    blocks = reps * count

    def sent(value, place):
        cols = lax.axis_size("col")
        pairs = []
        for col in range(cols):
            for r in range(reps):
                to_col, to_rep = place(col, r)
                pairs.append((col * reps + r, (to_col % cols) * reps + to_rep))
        return lax.ppermute(value, ("col", "rep"), pairs)

    def along_y(value):
        return sent(value, lambda col, r: (col, r ^ 2))

    def along_core(value):
        return sent(value, lambda col, r: (col, r ^ 1))

    def along_z(value):
        return sent(value, lambda col, r: (col + 2 * stride, r))

    def along_x(value):
        return sent(value, lambda col, r: (col + stride if (col // stride) % 2 == 0 else col - stride, r))

    vmem = pl.BlockSpec(memory_space=VMEM)
    smem = pl.BlockSpec(memory_space=SMEM)
    anywhere = pl.BlockSpec(memory_space=pl.ANY)

    codes = tile_blocks[0, :, :, 0] * 256 + tile_blocks[0, :, :, 1]
    alive = jnp.arange(slots, dtype=jnp.int32)[None, :] < tile_count[0][:, None]
    codes = jnp.where(alive, codes, -1)
    other_codes = along_core(codes)
    other_targets = along_core(targets)

    def gated(values, *tokens):
        return kernel_call(
            gate_kernel,
            "gate",
            0.3,
            out_shape=tuple(jax.ShapeDtypeStruct(v.shape, v.dtype) for v in values),
            in_specs=[anywhere] * (len(values) + len(tokens)),
            out_specs=(anywhere,) * len(values),
            input_output_aliases={i: i for i in range(len(values))},
        )(*values, *tokens)

    weights = kernel_call(
        weights_kernel,
        "row_weights",
        9,
        out_shape=jax.ShapeDtypeStruct((blocks, side), jnp.float32),
        grid=(offsets,),
        in_specs=[smem, smem, pl.BlockSpec((1, slots, side, side), lambda k: (k, 0, 0, 0))],
        out_specs=vmem,
        scratch_shapes=[VMEM((blocks + 1, side, side), jnp.float32)],
    )(codes, tile_count[0], pltpu.with_memory_space_constraint(dissim[0], HBM))
    lists = kernel_call(
        functools.partial(lists_kernel, stride, count),
        "sort_slots",
        2,
        out_shape=jax.ShapeDtypeStruct((len(STAGES), 2 * slots * (offsets - 1) + 128), jnp.int32),
        in_specs=[vmem],
        out_specs=vmem,
    )(jnp.concatenate([codes, other_codes], axis=1))
    def chosen(at_even, at_odd):
        return kernel_call(
            functools.partial(choose_kernel, stride),
            "choose",
            0.5,
            out_shape=VMEM(at_even.shape, at_even.dtype),
            in_specs=[vmem, vmem],
            out_specs=vmem,
        )(at_even, at_odd)

    def tiles(stage, sums, *places, tokens=()):
        first = sums is None
        points, layout, at = [], [], 0
        for choices in places:
            choices = [(None, choices)] if not isinstance(choices, dict) else list(choices.items())
            for parity, arrays in choices:
                start = at
                for array in arrays:
                    points.append(array)
                    layout.append((start, parity))
                    start += array.shape[0] // side
            at = start
        sums_shape = VMEM((blocks + 1, side, side), jnp.float32)
        out = kernel_call(
            functools.partial(stage_kernel, stage, first, layout, stride, len(tokens)),
            f"tiles_{stage}",
            1 + 2.0 * len(STAGES[stage]),
            out_shape=(sums_shape, sums_shape, VMEM((8, side), jnp.float32)),
            in_specs=[smem, vmem, vmem]
            + [vmem] * len(points)
            + [anywhere] * 2
            + [anywhere] * len(tokens)
            + ([] if first else [vmem, vmem]),
            out_specs=(vmem, vmem, vmem),
            input_output_aliases={} if first else {5 + len(points) + len(tokens) + i: i for i in range(2)},
            scratch_shapes=[
                VMEM((at, side, side), jnp.bfloat16),
                VMEM((at, side), jnp.float32),
                VMEM((2, GROUP, side, side), jnp.bfloat16),
                VMEM((GROUP, side, side), jnp.bfloat16),
                pltpu.SemaphoreType.DMA((2,)),
            ],
        )(lists, rows, norms, *points, targets, other_targets, *tokens, *([] if first else sums))
        return out[:2], out[2]

    p20 = along_z(coords)
    p01 = along_y(coords)
    a10 = along_x(coords)
    near_rows = along_core(coords)
    p20, p01, a10, weights = gated((p20, p01, a10, weights))
    r10 = along_x(chosen(p01, p20))
    p40 = along_z(p20)
    p21 = along_y(p20)
    far_rows = along_core(p01)
    rows, norms = kernel_call(
        rows_kernel,
        "row_operands",
        3,
        out_shape=(VMEM((blocks, side, side), jnp.bfloat16), VMEM((blocks, side, side), jnp.float32)),
        in_specs=[vmem] * 4,
        out_specs=(vmem, vmem),
    )(coords, near_rows, p01, far_rows)
    rows = pltpu.with_memory_space_constraint(rows, VMEM)
    norms = pltpu.with_memory_space_constraint(norms, VMEM)

    sums, token = tiles(0, None, (coords,), (p01,), (p20,))
    p40, p21, r10, a10, weights = gated((p40, p21, r10, a10, weights), token)
    p10 = chosen(r10, a10)
    p41 = along_y(p40)
    t21 = along_x(p21)
    p30 = along_z(p10)
    more_weights = along_core(weights)
    sums, token = tiles(1, sums, (p10,), (p21,), (p40,))
    half = jax.ShapeDtypeStruct((own_rows // 2, width), coords.dtype)
    upper, lower, weights = kernel_call(
        halves_kernel,
        "halves",
        0.5,
        out_shape=(half, half, jax.ShapeDtypeStruct(weights.shape, weights.dtype)),
        in_specs=[vmem] * 4 + [anywhere],
        out_specs=(vmem,) * 3,
    )(p41, t21, weights, more_weights, token)
    d31 = along_x(upper), along_z(lower)
    more_weights = along_y(weights)
    sums, token = tiles(2, sums, (p41,), (t21,), (p30,))
    sums, token = tiles(3, sums, {1: d31, 0: (r10,)}, tokens=(more_weights,))
    scale = kernel_call(
        scale_kernel,
        "row_scale",
        1,
        out_shape=jax.ShapeDtypeStruct((own_rows, side), jnp.float32),
        in_specs=[vmem, vmem],
        out_specs=vmem,
    )(weights, more_weights)

    sums = [pltpu.with_memory_space_constraint(value, VMEM) for value in sums]

    def pack_core(flip, name, points):
        return kernel_call(
            functools.partial(pack_core_kernel, flip),
            name,
            1,
            out_shape=jax.ShapeDtypeStruct((own_rows, side), jnp.float32),
            in_specs=[vmem] * 3,
            out_specs=vmem,
        )(*sums, points)

    got_far = along_core(pack_core(3, "pack_core_far", far_rows))
    to_far = kernel_call(
        pack_far_kernel,
        "pack_far",
        1.5,
        out_shape=jax.ShapeDtypeStruct((own_rows + count, side), jnp.bfloat16),
        in_specs=[vmem] * 5,
        out_specs=vmem,
    )(*sums, norms, got_far, p01)
    far = along_y(to_far)
    got_near = along_core(pack_core(1, "pack_core_near", near_rows))
    base = kernel_call(
        base_kernel,
        "own_rows",
        1.5,
        out_shape=jax.ShapeDtypeStruct((own_rows, side), jnp.float32),
        in_specs=[vmem] * 5,
        out_specs=vmem,
    )(*sums, got_near, scale, coords)
    return kernel_call(
        finish_kernel,
        "finish",
        1,
        out_shape=jax.ShapeDtypeStruct((own_rows, width), jnp.float32),
        in_specs=[vmem] * 4,
        out_specs=vmem,
    )(base, far, scale, coords)


def solution(mesh):
    in_specs = (
        P(("col", "rep"), None),
        P(("col", "rep"), None, None, None, None),
        P(("col", "rep"), None, None, None),
        P(("col", "rep"), None),
    )
    out_specs = P(("col", "rep"), None)
    return jax.shard_map(
        per_device, mesh=mesh, in_specs=in_specs, out_specs=out_specs, check_vma=False
    )
```

profile of v0, /device:TPU:0, one launch (start us, length us, event | category | flops | bytes accessed | tf_op | source)
XLA Modules:
  0.0 85.4 jit_solution(6065082734687473701)
XLA Ops:
  0.0 0.5 collective-permute-start.9
  0.5 2.6 %collective-permute-start.2 = (bf16[2048,128]{1,0:T(8,128)(2,1)}, bf16[2048,128]{1,0:T(8,128)(2,1)S(1)}, u32[]{:S(2)}, u32[]{:S(2)}) collective-permute-start(bf16[2048,128]{1,0:T(8,128)(2,1)} %points_ref.3), channel_id=1, source_target_pairs={{0,8},{1,9},{2,10},{3,11},{4,12},{5,13},{6,14},{7,15},{8,16},{9,17... | collective-permute-start | bytes 1572872 | tf_op jit(solution)/shard_map/ppermute | solution.py:336
  3.0 1.5 %collective-permute-start.3 = (bf16[2048,128]{1,0:T(8,128)(2,1)}, bf16[2048,128]{1,0:T(8,128)(2,1)S(1)}, u32[]{:S(2)}, u32[]{:S(2)}) collective-permute-start(bf16[2048,128]{1,0:T(8,128)(2,1)} %points_ref.3), channel_id=1, source_target_pairs={{0,2},{1,3},{2,0},{3,1},{4,6},{5,7},{6,4},{7,5},{8,10},{9,11},{10,... | collective-permute-start | bytes 1572872 | tf_op jit(solution)/shard_map/ppermute | solution.py:336
  4.5 1.5 %collective-permute-start.4 = (bf16[2048,128]{1,0:T(8,128)(2,1)}, bf16[2048,128]{1,0:T(8,128)(2,1)S(1)}, u32[]{:S(2)}, u32[]{:S(2)}) collective-permute-start(bf16[2048,128]{1,0:T(8,128)(2,1)} %points_ref.3), channel_id=1, source_target_pairs={{0,4},{1,5},{2,6},{3,7},{4,0},{5,1},{6,2},{7,3},{8,12},{9,13},{10,... | collective-permute-start | bytes 1572872 | tf_op jit(solution)/shard_map/ppermute | solution.py:336
  6.0 0.0 collective-permute-start.1
  6.0 0.8 fusion.2
  6.8 0.7 fusion.1.codes
  7.5 0.0 copy-start.1
  7.5 0.7 copy-done.1
  8.2 9.0 %row_weights.1.refs_3_ = f32[64,128]{1,0:T(8,128)S(1)} custom-call(s32[5,64]{1,0:T(8,128)S(1)} %fusion.1.codes, s32[5]{0:T(128)S(1)} %bitcast.8, bf16[5,64,128,128]{3,2,1,0:T(8,128)(2,1)} %bitcast.10), custom_call_target="tpu_custom_call" | custom-call | flops 2249999872 | bytes 6750000 | tf_op jit(solution)/shard_map/row_weights/pallas_call | solution.py:371
  17.2 0.0 copy-start
  17.3 0.6 collective-permute-done.2.refs_0_
  17.9 0.0 collective-permute-done.3.refs_1_
  17.9 0.7 collective-permute-done.4.refs_2_
  18.5 0.0 collective-permute-start.5
  18.5 0.5 collective-permute-start
  19.1 1.6 %collective-permute-start.6 = (bf16[2048,128]{1,0:T(8,128)(2,1)S(1)}, bf16[2048,128]{1,0:T(8,128)(2,1)S(1)}, u32[]{:S(2)}, u32[]{:S(2)}) collective-permute-start(bf16[2048,128]{1,0:T(8,128)(2,1)S(1)} %get-tuple-element.32.at_odd.rest_2_), channel_id=1, source_target_pairs={{0,8},{1,9},{2,10},{3,11},{4,12},{5,13},{6,14},{7,15},{8,16},{9,17... | collective-permute-start | bytes 1572872 | tf_op jit(solution)/shard_map/ppermute | solution.py:336
  20.7 0.0 collective-permute-done
  20.7 1.5 %collective-permute-start.8 = (bf16[2048,128]{1,0:T(8,128)(2,1)S(1)}, bf16[2048,128]{1,0:T(8,128)(2,1)S(1)}, u32[]{:S(2)}, u32[]{:S(2)}) collective-permute-start(bf16[2048,128]{1,0:T(8,128)(2,1)S(1)} %choose.2), channel_id=1, source_target_pairs={{0,4},{1,5},{2,6},{3,7},{4,0},{5,1},{6,2},{7,3},{8,12},{9,13},{10,... | collective-permute-start | bytes 1572872 | tf_op jit(solution)/shard_map/ppermute | solution.py:336
  22.2 0.0 collective-permute-done.1.q1.points_ref
  22.2 0.6 collective-permute-start.7
  22.9 0.1 pad_add_fusion.codes
  22.9 1.4 %sort_slots.1.lists = s32[4,640]{1,0:T(4,128)S(1)} custom-call(s32[5,128]{1,0:T(8,128)S(1)} %pad_add_fusion.codes), custom_call_target="tpu_custom_call" | custom-call | flops 500000000 | bytes 1500000 | tf_op jit(solution)/shard_map/sort_slots/pallas_call | solution.py:381
  24.3 0.0 collective-permute-done.5.q3.points_ref
  24.3 0.0 copy-done
  24.3 2.3 %row_operands.1 = (bf16[64,128,128]{2,1,0:T(8,128)(2,1)S(1)}, f32[64,128,128]{2,1,0:T(8,128)S(1)}) custom-call(bf16[2048,128]{1,0:T(8,128)(2,1)S(1)} %copy-done, bf16[2048,128]{1,0:T(8,128)(2,1)S(1)} %collective-permute-done.1.q1.points_ref, bf16[2048,128]{1,0:T(8,128)(2,1)S(1)} %get-tuple-element.29.q2.at_even.rest_1_.points_ref, ...), custom_call_target="tpu_custom_call" | custom-call | flops 750000000 | bytes 2250000 | tf_op jit(solution)/shard_map/row_operands/pallas_call | solution.py:443
  26.6 0.0 collective-permute-done.9.rest_4_
  26.7 7.9 %tiles_0.1 = (f32[65,128,128]{2,1,0:T(8,128)S(1)}, f32[65,128,128]{2,1,0:T(8,128)S(1)}, f32[8,128]{1,0:T(8,128)S(1)}) custom-call(s32[4,640]{1,0:T(4,128)S(1)} %sort_slots.1.lists, bf16[64,128,128]{2,1,0:T(8,128)(2,1)S(1)} %get-tuple-element.30.rows, f32[64,128,128]{2,1,0:T(8,128)S(1)} %get-tuple-element.31.norms, bf16[2048,128]{1,0:T(8,128)(2,1)S(1)} %copy-done, ...), custom_call_target="tpu_custom_call" | custom-call | flops 1750000000 | bytes 5250000 | tf_op jit(solution)/shard_map/tiles_0/pallas_call | solution.py:412
  34.5 0.0 collective-permute-done.8.refs_2_
  34.5 0.2 collective-permute-done.6.refs_0_
  34.8 0.9 %collective-permute-done.7.refs_1_ = bf16[2048,128]{1,0:T(8,128)(2,1)S(1)} collective-permute-done((bf16[2048,128]{1,0:T(8,128)(2,1)S(1)}, bf16[2048,128]{1,0:T(8,128)(2,1)S(1)}, u32[]{:S(2)}, u32[]{:S(2)}) %collective-permute-start.7) | collective-permute-done | bytes 524320 | tf_op jit(solution)/shard_map/ppermute | solution.py:336
  35.6 0.9 %collective-permute-start.10 = (bf16[2048,128]{1,0:T(8,128)(2,1)S(1)}, bf16[2048,128]{1,0:T(8,128)(2,1)S(1)}, u32[]{:S(2)}, u32[]{:S(2)}) collective-permute-start(bf16[2048,128]{1,0:T(8,128)(2,1)S(1)} %get-tuple-element.36.rest_2_), channel_id=1, source_target_pairs={{0,2},{1,3},{2,0},{3,1},{4,6},{5,7},{6,4},{7,5},{8,10},{9,11},{10,... | collective-permute-start | bytes 1572872 | tf_op jit(solution)/shard_map/ppermute | solution.py:336
  36.5 0.7 collective-permute-start.11
  37.3 1.1 %collective-permute-start.16 = (bf16[2048,128]{1,0:T(8,128)(2,1)S(1)}, bf16[2048,128]{1,0:T(8,128)(2,1)S(1)}, u32[]{:S(2)}, u32[]{:S(2)}) collective-permute-start(bf16[2048,128]{1,0:T(8,128)(2,1)S(1)} %choose.3.rest_0_), channel_id=1, source_target_pairs={{0,8},{1,9},{2,10},{3,11},{4,12},{5,13},{6,14},{7,15},{8,16},{9,17... | collective-permute-start | bytes 1572872 | tf_op jit(solution)/shard_map/ppermute | solution.py:336
  38.4 0.0 collective-permute-start.12
  38.4 5.3 %tiles_1.1 = (f32[65,128,128]{2,1,0:T(8,128)S(1)}, f32[65,128,128]{2,1,0:T(8,128)S(1)}, f32[8,128]{1,0:T(8,128)S(1)}) custom-call(s32[4,640]{1,0:T(4,128)S(1)} %sort_slots.1.lists, bf16[64,128,128]{2,1,0:T(8,128)(2,1)S(1)} %get-tuple-element.30.rows, f32[64,128,128]{2,1,0:T(8,128)S(1)} %get-tuple-element.31.norms, ...), custom_call_target="tpu_custom_call", output_to_operand_aliasing={{0}: (8, {}), {1}: (9, {})} | custom-call | flops 1750000000 | bytes 5250000 | tf_op jit(solution)/shard_map/tiles_1/pallas_call | solution.py:412
  43.6 0.0 collective-permute-done.12.more_weights
  43.6 4.5 %collective-permute-done.10.first.rest_0_ = bf16[2048,128]{1,0:T(8,128)(2,1)S(1)} collective-permute-done((bf16[2048,128]{1,0:T(8,128)(2,1)S(1)}, bf16[2048,128]{1,0:T(8,128)(2,1)S(1)}, u32[]{:S(2)}, u32[]{:S(2)}) %collective-permute-start.10) | collective-permute-done | bytes 524320 | tf_op jit(solution)/shard_map/ppermute | solution.py:336
  48.1 0.9 %collective-permute-done.11.second.rest_1_ = bf16[2048,128]{1,0:T(8,128)(2,1)S(1)} collective-permute-done((bf16[2048,128]{1,0:T(8,128)(2,1)S(1)}, bf16[2048,128]{1,0:T(8,128)(2,1)S(1)}, u32[]{:S(2)}, u32[]{:S(2)}) %collective-permute-start.11) | collective-permute-done | bytes 524320 | tf_op jit(solution)/shard_map/ppermute | solution.py:336
  49.1 1.0 %collective-permute-start.13 = (bf16[1024,128]{1,0:T(8,128)(2,1)S(1)}, bf16[1024,128]{1,0:T(8,128)(2,1)S(1)}, u32[]{:S(2)}, u32[]{:S(2)}) collective-permute-start(bf16[1024,128]{1,0:T(8,128)(2,1)S(1)} %get-tuple-element.44), channel_id=1, source_target_pairs={{0,4},{1,5},{2,6},{3,7},{4,0},{5,1},{6,2},{7,3},{8,12},{9,13},{10,... | collective-permute-start | bytes 786440 | tf_op jit(solution)/shard_map/ppermute | solution.py:336
  50.1 1.8 %collective-permute-start.14 = (bf16[1024,128]{1,0:T(8,128)(2,1)S(1)}, bf16[1024,128]{1,0:T(8,128)(2,1)S(1)}, u32[]{:S(2)}, u32[]{:S(2)}) collective-permute-start(bf16[1024,128]{1,0:T(8,128)(2,1)S(1)} %get-tuple-element.45), channel_id=1, source_target_pairs={{0,8},{1,9},{2,10},{3,11},{4,12},{5,13},{6,14},{7,15},{8,16},{9,17... | collective-permute-start | bytes 786440 | tf_op jit(solution)/shard_map/ppermute | solution.py:336
  51.9 1.7 %collective-permute-start.15 = (f32[64,128]{1,0:T(8,128)S(1)}, f32[64,128]{1,0:T(8,128)S(1)}, u32[]{:S(2)}, u32[]{:S(2)}) collective-permute-start(f32[64,128]{1,0:T(8,128)S(1)} %get-tuple-element.46.weights), channel_id=1, source_target_pairs={{0,2},{1,3},{2,0},{3,1},{4,6},{5,7},{6,4},{7,5},{8,10},{9,11},{10,... | collective-permute-start | bytes 98312 | tf_op jit(solution)/shard_map/ppermute | solution.py:336
  53.6 0.0 collective-permute-done.16.rest_2_
  53.6 8.0 %tiles_2.1 = (f32[65,128,128]{2,1,0:T(8,128)S(1)}, f32[65,128,128]{2,1,0:T(8,128)S(1)}, f32[8,128]{1,0:T(8,128)}) custom-call(s32[4,640]{1,0:T(4,128)S(1)} %sort_slots.1.lists, bf16[64,128,128]{2,1,0:T(8,128)(2,1)S(1)} %get-tuple-element.30.rows, f32[64,128,128]{2,1,0:T(8,128)S(1)} %get-tuple-element.31.norms, ...), custom_call_target="tpu_custom_call", output_to_operand_aliasing={{0}: (8, {}), {1}: (9, {})} | custom-call | flops 1750000000 | bytes 5250000 | tf_op jit(solution)/shard_map/tiles_2/pallas_call | solution.py:412
  61.6 0.0 collective-permute-done.15.rest_5_.more_weights
  61.6 0.0 collective-permute-done.13.rest_0_
  61.6 0.0 collective-permute-done.14.rest_1_
  61.6 4.6 %tiles_3.1 = (f32[65,128,128]{2,1,0:T(8,128)S(1)}, f32[65,128,128]{2,1,0:T(8,128)S(1)}, f32[8,128]{1,0:T(8,128)}) custom-call(s32[4,640]{1,0:T(4,128)S(1)} %sort_slots.1.lists, bf16[64,128,128]{2,1,0:T(8,128)(2,1)S(1)} %get-tuple-element.30.rows, f32[64,128,128]{2,1,0:T(8,128)S(1)} %get-tuple-element.31.norms, ...), custom_call_target="tpu_custom_call", output_to_operand_aliasing={{0}: (9, {}), {1}: (10, {})} | custom-call | flops 750000000 | bytes 2250000 | tf_op jit(solution)/shard_map/tiles_3/pallas_call | solution.py:412
  66.2 0.4 pack_core_far.1
  66.6 0.1 collective-permute-start.18
  66.6 0.4 pack_core_near.1
  67.0 0.6 collective-permute-start.17
  67.5 1.7 %collective-permute-done.18.got = f32[2048,128]{1,0:T(8,128)S(1)} collective-permute-done((f32[2048,128]{1,0:T(8,128)S(1)}, f32[2048,128]{1,0:T(8,128)S(1)}, u32[]{:S(2)}, u32[]{:S(2)}) %collective-permute-start.18) | collective-permute-done | bytes 1048608 | tf_op jit(solution)/shard_map/ppermute | solution.py:336
  69.3 0.7 pack_far.1
  69.9 0.1 collective-permute-start.19
  70.0 0.4 row_scale.1.scale
  70.4 0.4 collective-permute-done.17.near
  70.8 0.4 own_rows.1.base
  71.2 12.9 %collective-permute-done.19.far = bf16[2064,128]{1,0:T(8,128)(2,1)S(1)} collective-permute-done((bf16[2064,128]{1,0:T(8,128)(2,1)S(1)}, bf16[2064,128]{1,0:T(8,128)(2,1)S(1)}, u32[]{:S(2)}, u32[]{:S(2)}) %collective-permute-start.19) | collective-permute-done | bytes 528416 | tf_op jit(solution)/shard_map/ppermute | solution.py:336
  84.1 1.4 %finish.1 = f32[2048,128]{1,0:T(8,128)} custom-call(f32[2048,128]{1,0:T(8,128)S(1)} %own_rows.1.base, bf16[2064,128]{1,0:T(8,128)(2,1)S(1)} %collective-permute-done.19.far, f32[2048,128]{1,0:T(8,128)S(1)} %row_scale.1.scale, bf16[2048,128]{1,0:T(8,128)(2,1)S(1)} %copy-done), custom_call_target="tpu_custom_call" | custom-call | flops 250000000 | bytes 750000 | tf_op jit(solution)/shard_map/finish/pallas_call | solution.py:515
  (5 shorter events, 0.1 us)
Async XLA Ops:
  0.0 26.6 %collective-permute-start.9 = (bf16[320,128,128]{2,1,0:T(8,128)(2,1)}, bf16[320,128,128]{2,1,0:T(8,128)(2,1)}, u32[]{:S(2)}, u32[]{:S(2)}) collective-permute-start(bf16[320,128,128]{2,1,0:T(8,128)(2,1)} %bitcast.9), channel_id=1, source_target_pairs={{0,1},{1,0},{2,3},{3,2},{4,5},{5,4},{6,7},{7,6},{8,9},{9,8},{10,11... | collective-permute-start | bytes 31457288 | tf_op jit(solution)/shard_map/ppermute | solution.py:336
  0.5 17.4 %collective-permute-start.2 = (bf16[2048,128]{1,0:T(8,128)(2,1)}, bf16[2048,128]{1,0:T(8,128)(2,1)S(1)}, u32[]{:S(2)}, u32[]{:S(2)}) collective-permute-start(bf16[2048,128]{1,0:T(8,128)(2,1)} %points_ref.3), channel_id=1, source_target_pairs={{0,8},{1,9},{2,10},{3,11},{4,12},{5,13},{6,14},{7,15},{8,16},{9,17... | collective-permute-start | bytes 1572872 | tf_op jit(solution)/shard_map/ppermute | solution.py:336
  3.0 14.8 %collective-permute-start.3 = (bf16[2048,128]{1,0:T(8,128)(2,1)}, bf16[2048,128]{1,0:T(8,128)(2,1)S(1)}, u32[]{:S(2)}, u32[]{:S(2)}) collective-permute-start(bf16[2048,128]{1,0:T(8,128)(2,1)} %points_ref.3), channel_id=1, source_target_pairs={{0,2},{1,3},{2,0},{3,1},{4,6},{5,7},{6,4},{7,5},{8,10},{9,11},{10,... | collective-permute-start | bytes 1572872 | tf_op jit(solution)/shard_map/ppermute | solution.py:336
  4.5 14.0 %collective-permute-start.4 = (bf16[2048,128]{1,0:T(8,128)(2,1)}, bf16[2048,128]{1,0:T(8,128)(2,1)S(1)}, u32[]{:S(2)}, u32[]{:S(2)}) collective-permute-start(bf16[2048,128]{1,0:T(8,128)(2,1)} %points_ref.3), channel_id=1, source_target_pairs={{0,4},{1,5},{2,6},{3,7},{4,0},{5,1},{6,2},{7,3},{8,12},{9,13},{10,... | collective-permute-start | bytes 1572872 | tf_op jit(solution)/shard_map/ppermute | solution.py:336
  6.0 16.2 %collective-permute-start.1 = (bf16[2048,128]{1,0:T(8,128)(2,1)}, bf16[2048,128]{1,0:T(8,128)(2,1)S(1)}, u32[]{:S(2)}, u32[]{:S(2)}) collective-permute-start(bf16[2048,128]{1,0:T(8,128)(2,1)} %points_ref.3), channel_id=1, source_target_pairs={{0,1},{1,0},{2,3},{3,2},{4,5},{5,4},{6,7},{7,6},{8,9},{9,8},{10,11... | collective-permute-start | bytes 1572872 | tf_op jit(solution)/shard_map/ppermute | solution.py:336
  7.5 0.7 copy-start.1
  17.2 7.1 %copy-start = (bf16[2048,128]{1,0:T(8,128)(2,1)S(1)}, bf16[2048,128]{1,0:T(8,128)(2,1)}, u32[]{:S(2)}) copy-start(bf16[2048,128]{1,0:T(8,128)(2,1)} %points_ref.3) | copy-start | bytes 1572868
  18.5 5.8 %collective-permute-start.5 = (bf16[2048,128]{1,0:T(8,128)(2,1)S(1)}, bf16[2048,128]{1,0:T(8,128)(2,1)S(1)}, u32[]{:S(2)}, u32[]{:S(2)}) collective-permute-start(bf16[2048,128]{1,0:T(8,128)(2,1)S(1)} %get-tuple-element.29.q2.at_even.rest_1_.points_ref), channel_id=1, source_target_pairs={{0,1},{1,0},{2,3},{3,2},{4,5},{5,4},{6,7},{7,6},{8,9},{9,8},{10,11... | collective-permute-start | bytes 1572872 | tf_op jit(solution)/shard_map/ppermute | solution.py:336
  18.5 2.2 %collective-permute-start = (s32[5,64]{1,0:T(8,128)S(1)}, s32[5,64]{1,0:T(8,128)S(1)}, u32[]{:S(2)}, u32[]{:S(2)}) collective-permute-start(s32[5,64]{1,0:T(8,128)S(1)} %fusion.1.codes), channel_id=1, source_target_pairs={{0,1},{1,0},{2,3},{3,2},{4,5},{5,4},{6,7},{7,6},{8,9},{9,8},{10,11... | collective-permute-start | bytes 3848 | tf_op jit(solution)/shard_map/ppermute | solution.py:336
  19.1 15.7 %collective-permute-start.6 = (bf16[2048,128]{1,0:T(8,128)(2,1)S(1)}, bf16[2048,128]{1,0:T(8,128)(2,1)S(1)}, u32[]{:S(2)}, u32[]{:S(2)}) collective-permute-start(bf16[2048,128]{1,0:T(8,128)(2,1)S(1)} %get-tuple-element.32.at_odd.rest_2_), channel_id=1, source_target_pairs={{0,8},{1,9},{2,10},{3,11},{4,12},{5,13},{6,14},{7,15},{8,16},{9,17... | collective-permute-start | bytes 1572872 | tf_op jit(solution)/shard_map/ppermute | solution.py:336
  20.7 13.8 %collective-permute-start.8 = (bf16[2048,128]{1,0:T(8,128)(2,1)S(1)}, bf16[2048,128]{1,0:T(8,128)(2,1)S(1)}, u32[]{:S(2)}, u32[]{:S(2)}) collective-permute-start(bf16[2048,128]{1,0:T(8,128)(2,1)S(1)} %choose.2), channel_id=1, source_target_pairs={{0,4},{1,5},{2,6},{3,7},{4,0},{5,1},{6,2},{7,3},{8,12},{9,13},{10,... | collective-permute-start | bytes 1572872 | tf_op jit(solution)/shard_map/ppermute | solution.py:336
  22.2 13.4 %collective-permute-start.7 = (bf16[2048,128]{1,0:T(8,128)(2,1)S(1)}, bf16[2048,128]{1,0:T(8,128)(2,1)S(1)}, u32[]{:S(2)}, u32[]{:S(2)}) collective-permute-start(bf16[2048,128]{1,0:T(8,128)(2,1)S(1)} %get-tuple-element.32.at_odd.rest_2_), channel_id=1, source_target_pairs={{0,2},{1,3},{2,0},{3,1},{4,6},{5,7},{6,4},{7,5},{8,10},{9,11},{10,... | collective-permute-start | bytes 1572872 | tf_op jit(solution)/shard_map/ppermute | solution.py:336
  35.6 12.5 %collective-permute-start.10 = (bf16[2048,128]{1,0:T(8,128)(2,1)S(1)}, bf16[2048,128]{1,0:T(8,128)(2,1)S(1)}, u32[]{:S(2)}, u32[]{:S(2)}) collective-permute-start(bf16[2048,128]{1,0:T(8,128)(2,1)S(1)} %get-tuple-element.36.rest_2_), channel_id=1, source_target_pairs={{0,2},{1,3},{2,0},{3,1},{4,6},{5,7},{6,4},{7,5},{8,10},{9,11},{10,... | collective-permute-start | bytes 1572872 | tf_op jit(solution)/shard_map/ppermute | solution.py:336
  36.5 12.5 %collective-permute-start.11 = (bf16[2048,128]{1,0:T(8,128)(2,1)S(1)}, bf16[2048,128]{1,0:T(8,128)(2,1)S(1)}, u32[]{:S(2)}, u32[]{:S(2)}) collective-permute-start(bf16[2048,128]{1,0:T(8,128)(2,1)S(1)} %get-tuple-element.37.rest_1_), channel_id=1, source_target_pairs={{0,4},{1,5},{2,6},{3,7},{4,0},{5,1},{6,2},{7,3},{8,12},{9,13},{10,... | collective-permute-start | bytes 1572872 | tf_op jit(solution)/shard_map/ppermute | solution.py:336
  37.3 16.3 %collective-permute-start.16 = (bf16[2048,128]{1,0:T(8,128)(2,1)S(1)}, bf16[2048,128]{1,0:T(8,128)(2,1)S(1)}, u32[]{:S(2)}, u32[]{:S(2)}) collective-permute-start(bf16[2048,128]{1,0:T(8,128)(2,1)S(1)} %choose.3.rest_0_), channel_id=1, source_target_pairs={{0,8},{1,9},{2,10},{3,11},{4,12},{5,13},{6,14},{7,15},{8,16},{9,17... | collective-permute-start | bytes 1572872 | tf_op jit(solution)/shard_map/ppermute | solution.py:336
  38.4 5.3 %collective-permute-start.12 = (f32[64,128]{1,0:T(8,128)S(1)}, f32[64,128]{1,0:T(8,128)S(1)}, u32[]{:S(2)}, u32[]{:S(2)}) collective-permute-start(f32[64,128]{1,0:T(8,128)S(1)} %get-tuple-element.38.weights), channel_id=1, source_target_pairs={{0,1},{1,0},{2,3},{3,2},{4,5},{5,4},{6,7},{7,6},{8,9},{9,8},{10,11... | collective-permute-start | bytes 98312 | tf_op jit(solution)/shard_map/ppermute | solution.py:336
  49.1 12.4 %collective-permute-start.13 = (bf16[1024,128]{1,0:T(8,128)(2,1)S(1)}, bf16[1024,128]{1,0:T(8,128)(2,1)S(1)}, u32[]{:S(2)}, u32[]{:S(2)}) collective-permute-start(bf16[1024,128]{1,0:T(8,128)(2,1)S(1)} %get-tuple-element.44), channel_id=1, source_target_pairs={{0,4},{1,5},{2,6},{3,7},{4,0},{5,1},{6,2},{7,3},{8,12},{9,13},{10,... | collective-permute-start | bytes 786440 | tf_op jit(solution)/shard_map/ppermute | solution.py:336
  50.1 11.4 %collective-permute-start.14 = (bf16[1024,128]{1,0:T(8,128)(2,1)S(1)}, bf16[1024,128]{1,0:T(8,128)(2,1)S(1)}, u32[]{:S(2)}, u32[]{:S(2)}) collective-permute-start(bf16[1024,128]{1,0:T(8,128)(2,1)S(1)} %get-tuple-element.45), channel_id=1, source_target_pairs={{0,8},{1,9},{2,10},{3,11},{4,12},{5,13},{6,14},{7,15},{8,16},{9,17... | collective-permute-start | bytes 786440 | tf_op jit(solution)/shard_map/ppermute | solution.py:336
  51.9 9.7 %collective-permute-start.15 = (f32[64,128]{1,0:T(8,128)S(1)}, f32[64,128]{1,0:T(8,128)S(1)}, u32[]{:S(2)}, u32[]{:S(2)}) collective-permute-start(f32[64,128]{1,0:T(8,128)S(1)} %get-tuple-element.46.weights), channel_id=1, source_target_pairs={{0,2},{1,3},{2,0},{3,1},{4,6},{5,7},{6,4},{7,5},{8,10},{9,11},{10,... | collective-permute-start | bytes 98312 | tf_op jit(solution)/shard_map/ppermute | solution.py:336
  66.6 2.7 %collective-permute-start.18 = (f32[2048,128]{1,0:T(8,128)S(1)}, f32[2048,128]{1,0:T(8,128)S(1)}, u32[]{:S(2)}, u32[]{:S(2)}) collective-permute-start(f32[2048,128]{1,0:T(8,128)S(1)} %pack_core_far.1), channel_id=1, source_target_pairs={{0,1},{1,0},{2,3},{3,2},{4,5},{5,4},{6,7},{7,6},{8,9},{9,8},{10,11... | collective-permute-start | bytes 3145736 | tf_op jit(solution)/shard_map/ppermute | solution.py:336
  67.0 3.8 %collective-permute-start.17 = (f32[2048,128]{1,0:T(8,128)S(1)}, f32[2048,128]{1,0:T(8,128)S(1)}, u32[]{:S(2)}, u32[]{:S(2)}) collective-permute-start(f32[2048,128]{1,0:T(8,128)S(1)} %pack_core_near.1), channel_id=1, source_target_pairs={{0,1},{1,0},{2,3},{3,2},{4,5},{5,4},{6,7},{7,6},{8,9},{9,8},{10,11... | collective-permute-start | bytes 3145736 | tf_op jit(solution)/shard_map/ppermute | solution.py:336
  69.9 14.1 %collective-permute-start.19 = (bf16[2064,128]{1,0:T(8,128)(2,1)S(1)}, bf16[2064,128]{1,0:T(8,128)(2,1)S(1)}, u32[]{:S(2)}, u32[]{:S(2)}) collective-permute-start(bf16[2064,128]{1,0:T(8,128)(2,1)S(1)} %pack_far.1), channel_id=1, source_target_pairs={{0,2},{1,3},{2,0},{3,1},{4,6},{5,7},{6,4},{7,5},{8,10},{9,11},{10,... | collective-permute-start | bytes 1585160 | tf_op jit(solution)/shard_map/ppermute | solution.py:336
where the time goes:
time: 85.4 us
  Pallas kernels  42 us (49%)
  waiting for transfers between devices  22.9 us (27%)
  starting transfers between devices  18.1 us (21%)
  local copies, waits for them, and re-layouts  1.43 us (2%)
    pallas_call x4, Pallas kernels, tiles(): kernel_call(functools.partial(stage_kernel, stage, first, layout, stride,...  25.7 us
    ppermute x20, waiting for transfers between devices, sent(): return lax.ppermute(value, ('col', 'rep'), pairs)  22.9 us
    ppermute x20, starting transfers between devices, sent(): return lax.ppermute(value, ('col', 'rep'), pairs)  18.1 us
    pallas_call x1, Pallas kernels, per_device(): kernel_call(weights_kernel, 'row_weights', 9, out_shape=jax.ShapeDtypeStr...  9.04 us
    pallas_call x1, Pallas kernels, per_device(): kernel_call(rows_kernel, 'row_operands', 3, out_shape=(VMEM((blocks, side...  2.31 us
  transfers between devices with their start and end apart: 20, of which 9 were waited for; matrix products, arithmetic and copies ran while one was open for 2% of the time, Pallas kernels for 42%

commit v1 on v0

--- a/solution.py
+++ b/solution.py
@@ -12,11 +12,13 @@
 COST = 0.25
 VMEM_LIMIT = 34 * 1024 * 1024
 VMEM, SMEM, HBM = pltpu.VMEM, pltpu.SMEM, pltpu.HBM
+ALL, FAR, NEAR = None, True, False
 STAGES = (
-    ((0, 0), (1, 1), (4, 4)),
-    ((2, 2), (5, 5), (8, 8)),
-    ((9, 9), (3, 7), (6, 6)),
-    ((7, 3),),
+    (((0, 0), (1, 1), (4, 4)), ALL),
+    (((2, 2), (5, 5), (8, 8)), ALL),
+    (((9, 9), (3, 7), (6, 6)), FAR),
+    (((7, 3),), FAR),
+    (((9, 9), (3, 7), (6, 6), (7, 3)), NEAR),
 )
 
 
@@ -32,6 +34,13 @@
     return lax.broadcasted_iota(jnp.int32, (side, side), 0) == lanes_of((side, side))
 
 
+def split_three(value):
+    high = value.astype(jnp.bfloat16)
+    rest = value - high.astype(jnp.float32)
+    middle = rest.astype(jnp.bfloat16)
+    return high, middle, (rest - middle.astype(jnp.float32)).astype(jnp.bfloat16)
+
+
 def row_of(column):
     return jnp.sum(jnp.where(diagonal(column.shape[0]), column, 0.0), axis=0, keepdims=True)
 
@@ -40,16 +49,16 @@
     return jnp.sum(jnp.where(diagonal(row.shape[1]), row, 0.0), axis=1, keepdims=True)
 
 
-def lists_kernel(stride, per_quarter, codes, out):
+def lists_kernel(stride, per_quarter, codes, *outs):
     rep, even = place_of_device(stride)
     core, mine = rep & 1, lax.shift_right_arithmetic(rep, 1)
     offsets, width = codes.shape
-    room = out.shape[1] - 128
+    room = outs[0].shape[1] - 128
     lanes = lanes_of((1, width))
     later = lax.broadcasted_iota(jnp.int32, (width, width), 0) <= lanes_of((width, width))
     later = jnp.where(later, 1.0, 0.0).astype(jnp.bfloat16)
     place_of = lax.broadcasted_iota(jnp.int32, (room, width), 0).astype(jnp.float32) + 1.0
-    for stage, arrays in enumerate(STAGES):
+    for stage, (arrays, side_of_rows) in enumerate(STAGES):
         before = jnp.zeros((1, 1), jnp.float32)
         listed = jnp.zeros((32, room), jnp.float32)
         for offset in range(offsets):
@@ -58,16 +67,19 @@
                 continue
             code = codes[offset : offset + 1, :]
             row, col = lax.shift_right_arithmetic(code, 8), code & 255
-            quarter = jnp.zeros_like(col)
+            quarter, row_half = jnp.zeros_like(col), jnp.where(row >= 2 * per_quarter, 1, 0)
             for edge in range(1, 4):
                 quarter += jnp.where(col >= edge * per_quarter, 1, 0)
+            live = code >= 0
+            if side_of_rows is not ALL:
+                live = live & ((row_half != mine) if side_of_rows else (row_half == mine))
             match = jnp.zeros((1, width), jnp.float32)
             column = (col - quarter * per_quarter).astype(jnp.float32)
             for index, at_even, at_odd in here:
                 piece = jnp.where(even, at_even, at_odd)
                 wanted = jnp.bitwise_xor(mine, piece & 1) * 2 + core
                 wanted = jnp.where(lax.shift_right_arithmetic(piece, 1) == offset, wanted, -1)
-                hit = jnp.where((code >= 0) & (quarter == wanted), 1.0, 0.0)
+                hit = jnp.where(live & (quarter == wanted), 1.0, 0.0)
                 match += hit
                 column += hit * (index * per_quarter)
             found = before + jnp.dot(
@@ -84,8 +96,8 @@
         lane, row, column, offset = listed[0:1], listed[8:9], listed[16:17], listed[24:25]
         slots = width // 2
         tile = offset * slots + lane + jnp.where(lane >= slots, (offsets - 1) * slots, 0)
-        out[stage : stage + 1, :room] = tile * 65536 + row * 256 + column
-        out[stage : stage + 1, room:] = jnp.broadcast_to(before.astype(jnp.int32), (1, 128))
+        outs[stage][:, :room] = tile * 65536 + row * 256 + column
+        outs[stage][:, room:] = jnp.broadcast_to(before.astype(jnp.int32), (1, 128))
 
 
 def weights_kernel(codes, counts, targets, out, sums):
@@ -118,16 +130,6 @@
         lax.fori_loop(0, blocks // 8, close, 0)
 
 
-def scale_kernel(weights, more_weights, out):
-    count = weights.shape[0] // 4
-    side = weights.shape[1]
-    own = pl.ds(pl.multiple_of(lax.axis_index("rep") * count, count), count)
-    own = weights[own, :] + more_weights[own, :]
-    for block in range(count):
-        total = column_of(own[block : block + 1, :])
-        out[block * side : (block + 1) * side, :] = jnp.broadcast_to(1.0 / (total + 1.0), (side, side))
-
-
 def rows_kernel(q0, q1, q2, q3, out, norms):
     side = out.shape[1]
     count = q0.shape[0] // side
@@ -144,7 +146,7 @@
         lax.fori_loop(0, count, visit, 0, unroll=4)
 
 
-def stage_kernel(stage, first, layout, stride, tokens, lists, rows, norms, *rest):
+def stage_kernel(first, layout, stride, tokens, lists, rows, norms, *rest):
     parts = len(layout)
     points_refs, (own, other), rest = rest[:parts], rest[parts : parts + 2], rest[parts + 2 :]
     rest = rest[tokens:] if first else rest[tokens + 2 :]
@@ -153,12 +155,12 @@
     side = rows.shape[1]
     tiles = own.shape[0]
     dummy = pulled.shape[0] - 1
-    total = lists[stage, lists.shape[1] - 1]
+    total = lists[0, lists.shape[1] - 1]
     groups = (total + GROUP - 1) // GROUP
     token[...] = jnp.zeros_like(token)
 
     def entry(index):
-        return lists[stage, jnp.minimum(index, total - 1)]
+        return lists[0, jnp.minimum(index, total - 1)]
 
     def fetch(group, slot):
         for unit in range(GROUP):
@@ -234,24 +236,36 @@
     pass
 
 
-def halves_kernel(first, second, weights, more_weights, *rest):
-    upper, lower, total = rest[-3:]
-    half = upper.shape[0]
-    upper[...] = first[:half, :]
-    lower[...] = second[half:, :]
-    total[...] = weights[...] + more_weights[...]
-
-
-def choose_kernel(stride, at_even, at_odd, out):
+def second_round_kernel(stride, weights, early, near, far, *refs):
+    near_out, far_out, across = refs[-3:]
     even = place_of_device(stride)[1]
+    near_out[...] = near[...]
+    far_out[...] = far[...]
 
     @pl.when(even)
     def _():
-        out[...] = at_even[...]
+        across[...] = near[...]
 
     @pl.when(jnp.logical_not(even))
     def _():
-        out[...] = at_odd[...]
+        across[...] = far[...]
+
+
+def third_round_kernel(stride, at_even, at_odd, first, second, *refs):
+    chosen, outs = refs[-5], refs[-4:]
+    even = place_of_device(stride)[1]
+    for index, whole in enumerate((first, second)):
+        half = whole.shape[0] // 2
+        outs[2 * index][...] = whole[:half, :]
+        outs[2 * index + 1][...] = whole[half:, :]
+
+    @pl.when(even)
+    def _():
+        chosen[...] = at_even[...]
+
+    @pl.when(jnp.logical_not(even))
+    def _():
+        chosen[...] = at_odd[...]
 
 
 def drift(pulled, summed, block, points):
@@ -267,7 +281,7 @@
         out[rows, :] = drift(pulled, summed, base + block, points_ref[rows, :].astype(jnp.float32))
 
 
-def pack_far_kernel(pulled, summed, norms, got, points_ref, out):
+def pack_far_kernel(pulled, summed, norms, weights, more_weights, got, points_ref, out):
     side = pulled.shape[1]
     count = (pulled.shape[0] - 1) // 4
     base = jnp.bitwise_xor(lax.axis_index("rep"), 2) * count
@@ -281,10 +295,34 @@
         share = (along * pltpu.reciprocal(norms[base + block] - (1.0 - 1e-6), approx=True)).astype(jnp.bfloat16).astype(jnp.float32)
         out[rows, :] = (total - share * points).astype(jnp.bfloat16)
         shares.append(jnp.sum(jnp.where(diagonal(side), share, 0.0), axis=0, keepdims=True))
-    out[count * side :, :] = jnp.concatenate(shares, axis=0).astype(jnp.bfloat16)
-
-
-def base_kernel(pulled, summed, near, scale, points_ref, out):
+    at = count * side
+    out[at : at + count, :] = jnp.concatenate(shares, axis=0).astype(jnp.bfloat16)
+    theirs = pl.ds(pl.multiple_of(base, count), count)
+    for part in split_three(weights[theirs, :] + more_weights[theirs, :]):
+        at += count
+        out[at : at + count, :] = part
+
+
+def from_far_kernel(weights, more_weights, far, points_ref, out, scale):
+    side = weights.shape[1]
+    count = weights.shape[0] // 4
+    at = count * side
+    shares = far[at : at + count, :].astype(jnp.float32)
+    own = pl.ds(pl.multiple_of(lax.axis_index("rep") * count, count), count)
+    total_weights = weights[own, :] + more_weights[own, :]
+    for part in range(1, 4):
+        total_weights += far[at + part * count : at + (part + 1) * count, :].astype(jnp.float32)
+    factors = 1.0 / (total_weights + 1.0)
+    for block in range(count):
+        rows = slice(block * side, (block + 1) * side)
+        points = points_ref[rows, :].astype(jnp.float32)
+        factor = jnp.broadcast_to(column_of(factors[block : block + 1, :]), (side, side))
+        total = far[rows, :].astype(jnp.float32) + column_of(shares[block : block + 1, :]) * points
+        scale[rows, :] = factor
+        out[rows, :] = points + factor * total
+
+
+def finish_kernel(moved, pulled, summed, near, scale, points_ref, out):
     side = pulled.shape[1]
     count = (pulled.shape[0] - 1) // 4
     base = lax.axis_index("rep") * count
@@ -292,17 +330,7 @@
         rows = slice(block * side, (block + 1) * side)
         points = points_ref[rows, :].astype(jnp.float32)
         total = drift(pulled, summed, base + block, points) + near[rows, :]
-        out[rows, :] = points + scale[rows, :] * total
-
-
-def finish_kernel(base, far, scale, points_ref, out):
-    count, side = far.shape[0] - points_ref.shape[0], far.shape[1]
-    shares = far[count * side :, :].astype(jnp.float32)
-    for block in range(count):
-        rows = slice(block * side, (block + 1) * side)
-        points = points_ref[rows, :].astype(jnp.float32)
-        total = far[rows, :].astype(jnp.float32) + column_of(shares[block : block + 1, :]) * points
-        out[rows, :] = base[rows, :] + scale[rows, :] * total
+        out[rows, :] = moved[rows, :] + scale[rows, :] * total
 
 
 def kernel_call(body, name, cost, **options):
@@ -382,20 +410,10 @@
         functools.partial(lists_kernel, stride, count),
         "sort_slots",
         2,
-        out_shape=jax.ShapeDtypeStruct((len(STAGES), 2 * slots * (offsets - 1) + 128), jnp.int32),
+        out_shape=(jax.ShapeDtypeStruct((1, 2 * slots * (offsets - 1) + 128), jnp.int32),) * len(STAGES),
         in_specs=[vmem],
-        out_specs=vmem,
+        out_specs=(vmem,) * len(STAGES),
     )(jnp.concatenate([codes, other_codes], axis=1))
-    def chosen(at_even, at_odd):
-        return kernel_call(
-            functools.partial(choose_kernel, stride),
-            "choose",
-            0.5,
-            out_shape=VMEM(at_even.shape, at_even.dtype),
-            in_specs=[vmem, vmem],
-            out_specs=vmem,
-        )(at_even, at_odd)
-
     def tiles(stage, sums, *places, tokens=()):
         first = sums is None
         points, layout, at = [], [], 0
@@ -410,9 +428,9 @@
             at = start
         sums_shape = VMEM((blocks + 1, side, side), jnp.float32)
         out = kernel_call(
-            functools.partial(stage_kernel, stage, first, layout, stride, len(tokens)),
+            functools.partial(stage_kernel, first, layout, stride, len(tokens)),
             f"tiles_{stage}",
-            1 + 2.0 * len(STAGES[stage]),
+            0.05 if STAGES[stage][1] is NEAR else 1 + 2.0 * len(STAGES[stage][0]),
             out_shape=(sums_shape, sums_shape, VMEM((8, side), jnp.float32)),
             in_specs=[smem, vmem, vmem]
             + [vmem] * len(points)
@@ -428,18 +446,27 @@
                 VMEM((GROUP, side, side), jnp.bfloat16),
                 pltpu.SemaphoreType.DMA((2,)),
             ],
-        )(lists, rows, norms, *points, targets, other_targets, *tokens, *([] if first else sums))
+        )(lists[stage], rows, norms, *points, targets, other_targets, *tokens, *([] if first else sums))
         return out[:2], out[2]
 
     p20 = along_z(coords)
     p01 = along_y(coords)
     a10 = along_x(coords)
     near_rows = along_core(coords)
-    p20, p01, a10, weights = gated((p20, p01, a10, weights))
-    r10 = along_x(chosen(p01, p20))
+    whole = jax.ShapeDtypeStruct((own_rows, width), coords.dtype)
+    p01, p20, across = kernel_call(
+        functools.partial(second_round_kernel, stride),
+        "second_round",
+        0.5,
+        out_shape=(whole,) * 3,
+        in_specs=[anywhere] * 2 + [vmem] * 2,
+        out_specs=(vmem,) * 3,
+    )(weights, a10, p01, p20)
     p40 = along_z(p20)
     p21 = along_y(p20)
+    r10 = along_x(across)
     far_rows = along_core(p01)
+    more_weights = along_core(weights)
     rows, norms = kernel_call(
         rows_kernel,
         "row_operands",
@@ -452,37 +479,26 @@
     norms = pltpu.with_memory_space_constraint(norms, VMEM)
 
     sums, token = tiles(0, None, (coords,), (p01,), (p20,))
-    p40, p21, r10, a10, weights = gated((p40, p21, r10, a10, weights), token)
-    p10 = chosen(r10, a10)
-    p41 = along_y(p40)
-    t21 = along_x(p21)
+    half = jax.ShapeDtypeStruct((own_rows // 2, width), coords.dtype)
+    p10, p21a, p21b, p40a, p40b = kernel_call(
+        functools.partial(third_round_kernel, stride),
+        "third_round",
+        0.5,
+        out_shape=(whole,) + (half,) * 4,
+        in_specs=[vmem] * 4 + [anywhere] * 2,
+        out_specs=(vmem,) * 5,
+    )(r10, a10, p21, p40, more_weights, token)
+    p41a = along_y(p40a)
+    t21b = along_x(p21b)
     p30 = along_z(p10)
-    more_weights = along_core(weights)
+    p41b = along_y(p40b)
+    t21a = along_x(p21a)
     sums, token = tiles(1, sums, (p10,), (p21,), (p40,))
-    half = jax.ShapeDtypeStruct((own_rows // 2, width), coords.dtype)
-    upper, lower, weights = kernel_call(
-        halves_kernel,
-        "halves",
-        0.5,
-        out_shape=(half, half, jax.ShapeDtypeStruct(weights.shape, weights.dtype)),
-        in_specs=[vmem] * 4 + [anywhere],
-        out_specs=(vmem,) * 3,
-    )(p41, t21, weights, more_weights, token)
-    d31 = along_x(upper), along_z(lower)
-    more_weights = along_y(weights)
-    sums, token = tiles(2, sums, (p41,), (t21,), (p30,))
-    sums, token = tiles(3, sums, {1: d31, 0: (r10,)}, tokens=(more_weights,))
-    scale = kernel_call(
-        scale_kernel,
-        "row_scale",
-        1,
-        out_shape=jax.ShapeDtypeStruct((own_rows, side), jnp.float32),
-        in_specs=[vmem, vmem],
-        out_specs=vmem,
-    )(weights, more_weights)
-
-    sums = [pltpu.with_memory_space_constraint(value, VMEM) for value in sums]
-
+    p41a, t21b = gated((p41a, t21b), token)
+    d31 = along_x(p41a), along_z(t21b)
+    last = {1: d31, 0: (r10,)}
+    sums, token = tiles(2, sums, (p41a, p41b), (t21a, t21b), (p30,))
+    sums, token = tiles(3, sums, last)
     def pack_core(flip, name, points):
         return kernel_call(
             functools.partial(pack_core_kernel, flip),
@@ -493,33 +509,36 @@
             out_specs=vmem,
         )(*sums, points)
 
+    sums = [pltpu.with_memory_space_constraint(value, VMEM) for value in sums]
     got_far = along_core(pack_core(3, "pack_core_far", far_rows))
     to_far = kernel_call(
         pack_far_kernel,
         "pack_far",
         1.5,
-        out_shape=jax.ShapeDtypeStruct((own_rows + count, side), jnp.bfloat16),
-        in_specs=[vmem] * 5,
+        out_shape=jax.ShapeDtypeStruct((own_rows + 4 * count, side), jnp.bfloat16),
+        in_specs=[vmem] * 7,
         out_specs=vmem,
-    )(*sums, norms, got_far, p01)
+    )(*sums, norms, weights, more_weights, got_far, p01)
     far = along_y(to_far)
+    sums, token = tiles(4, sums, (p41a, p41b), (t21a, t21b), (p30,), last, tokens=(to_far,))
+    sums = [pltpu.with_memory_space_constraint(value, VMEM) for value in sums]
     got_near = along_core(pack_core(1, "pack_core_near", near_rows))
-    base = kernel_call(
-        base_kernel,
-        "own_rows",
-        1.5,
-        out_shape=jax.ShapeDtypeStruct((own_rows, side), jnp.float32),
-        in_specs=[vmem] * 5,
-        out_specs=vmem,
-    )(*sums, got_near, scale, coords)
+    moved, scale = kernel_call(
+        from_far_kernel,
+        "from_far",
+        80,
+        out_shape=(jax.ShapeDtypeStruct((own_rows, side), jnp.float32),) * 2,
+        in_specs=[vmem] * 4,
+        out_specs=(vmem,) * 2,
+    )(weights, more_weights, far, coords)
     return kernel_call(
         finish_kernel,
         "finish",
         1,
         out_shape=jax.ShapeDtypeStruct((own_rows, width), jnp.float32),
-        in_specs=[vmem] * 4,
+        in_specs=[vmem] * 6,
         out_specs=vmem,
-    )(base, far, scale, coords)
+    )(moved, *sums, got_near, scale, coords)
 
 
 def solution(mesh):

time: 85.4 us -> 83.8 us (0.981); the launches traced: 85.4 us -> 82.8 us
  waiting for transfers between devices: 22.9 us -> 11.7 us
  Pallas kernels: 42 us -> 52.1 us
  starting transfers between devices: 18.1 us -> 16.4 us
    ppermute x20 -> x21, waiting for transfers between devices: 22.9 us -> 11.7 us  [sent(): return lax.ppermute(value, ('col', 'rep'), pairs)]
    pallas_call x9 -> x8, Pallas kernels: 26.6 us -> 36.1 us  [the longest x5 35.2 us: tiles(): kernel_call(functools.partial(stage_kernel, first, layout, stride, len(to...]
    ppermute x20 -> x21, starting transfers between devices: 18.1 us -> 16.4 us  [sent(): return lax.ppermute(value, ('col', 'rep'), pairs)]
  transfers between devices with their start and end apart: 20 -> 21, of which waited for: 9 -> 7; matrix products, arithmetic and copies ran while one was open for 2% -> 2% of each run, Pallas kernels for 42% -> 56%
where the time goes in v1:
time: 83.8 us; the launch traced here: 82.8 us
  Pallas kernels  52.1 us (62%)
  starting transfers between devices  16.4 us (20%)
  waiting for transfers between devices  11.7 us (14%)
  local copies, waits for them, and re-layouts  1.43 us (2%)
    pallas_call x5, Pallas kernels, tiles(): kernel_call(functools.partial(stage_kernel, first, layout, stride, len(to...  35.2 us
    ppermute x21, starting transfers between devices, sent(): return lax.ppermute(value, ('col', 'rep'), pairs)  16.4 us
    ppermute x21, waiting for transfers between devices, sent(): return lax.ppermute(value, ('col', 'rep'), pairs)  11.7 us
    pallas_call x1, Pallas kernels, per_device(): kernel_call(weights_kernel, 'row_weights', 9, out_shape=jax.ShapeDtypeStr...  9.1 us
    pallas_call x1, Pallas kernels, per_device(): kernel_call(rows_kernel, 'row_operands', 3, out_shape=(VMEM((blocks, side...  2.31 us
    pallas_call x1, Pallas kernels, per_device(): kernel_call(functools.partial(lists_kernel, stride, count), 'sort_slots',...  1.77 us
  transfers between devices with their start and end apart: 21, of which 7 were waited for; matrix products, arithmetic and copies ran while one was open for 2% of the time, Pallas kernels for 56%

profile of v1, /device:TPU:0, one launch (start us, length us, event | category | flops | bytes accessed | tf_op | source)
XLA Modules:
  0.0 82.8 jit_solution(15098612592407752856)
XLA Ops:
  0.0 0.5 collective-permute-start.10
  0.5 2.6 %collective-permute-start.5 = (bf16[2048,128]{1,0:T(8,128)(2,1)}, bf16[2048,128]{1,0:T(8,128)(2,1)S(1)}, u32[]{:S(2)}, u32[]{:S(2)}) collective-permute-start(bf16[2048,128]{1,0:T(8,128)(2,1)} %points_ref.3), channel_id=1, source_target_pairs={{0,8},{1,9},{2,10},{3,11},{4,12},{5,13},{6,14},{7,15},{8,16},{9,17... | collective-permute-start | bytes 1572872 | tf_op jit(solution)/shard_map/ppermute | solution.py:364
  3.0 1.5 %collective-permute-start.4 = (bf16[2048,128]{1,0:T(8,128)(2,1)}, bf16[2048,128]{1,0:T(8,128)(2,1)S(1)}, u32[]{:S(2)}, u32[]{:S(2)}) collective-permute-start(bf16[2048,128]{1,0:T(8,128)(2,1)} %points_ref.3), channel_id=1, source_target_pairs={{0,2},{1,3},{2,0},{3,1},{4,6},{5,7},{6,4},{7,5},{8,10},{9,11},{10,... | collective-permute-start | bytes 1572872 | tf_op jit(solution)/shard_map/ppermute | solution.py:364
  4.5 1.5 %collective-permute-start.3 = (bf16[2048,128]{1,0:T(8,128)(2,1)}, bf16[2048,128]{1,0:T(8,128)(2,1)S(1)}, u32[]{:S(2)}, u32[]{:S(2)}) collective-permute-start(bf16[2048,128]{1,0:T(8,128)(2,1)} %points_ref.3), channel_id=1, source_target_pairs={{0,4},{1,5},{2,6},{3,7},{4,0},{5,1},{6,2},{7,3},{8,12},{9,13},{10,... | collective-permute-start | bytes 1572872 | tf_op jit(solution)/shard_map/ppermute | solution.py:364
  6.0 0.0 collective-permute-start.2
  6.0 0.8 fusion.2
  6.8 0.7 fusion.1.codes
  7.5 0.0 copy-start.1
  7.5 0.7 copy-done.1
  8.2 0.0 copy-start
  8.2 9.1 %row_weights.1.weights = f32[64,128]{1,0:T(8,128)S(1)} custom-call(s32[5,64]{1,0:T(8,128)S(1)} %fusion.1.codes, s32[5]{0:T(128)S(1)} %bitcast.8, bf16[5,64,128,128]{3,2,1,0:T(8,128)(2,1)} %bitcast.10), custom_call_target="tpu_custom_call" | custom-call | flops 2249999872 | bytes 6750000 | tf_op jit(solution)/shard_map/row_weights/pallas_call | solution.py:399
  17.3 0.6 collective-permute-done.5.far
  17.9 0.0 collective-permute-done.4.near
  17.9 0.7 collective-permute-done.3.early.at_odd
  18.5 0.1 second_round.1
  18.6 0.1 collective-permute-start.6
  18.7 0.5 collective-permute-start.1
  19.2 1.5 %collective-permute-start.7 = (bf16[2048,128]{1,0:T(8,128)(2,1)S(1)}, bf16[2048,128]{1,0:T(8,128)(2,1)S(1)}, u32[]{:S(2)}, u32[]{:S(2)}) collective-permute-start(bf16[2048,128]{1,0:T(8,128)(2,1)S(1)} %get-tuple-element.40), channel_id=1, source_target_pairs={{0,4},{1,5},{2,6},{3,7},{4,0},{5,1},{6,2},{7,3},{8,12},{9,13},{10,... | collective-permute-start | bytes 1572872 | tf_op jit(solution)/shard_map/ppermute | solution.py:364
  20.7 0.0 collective-permute-done.1
  20.7 1.6 %collective-permute-start.9 = (bf16[2048,128]{1,0:T(8,128)(2,1)S(1)}, bf16[2048,128]{1,0:T(8,128)(2,1)S(1)}, u32[]{:S(2)}, u32[]{:S(2)}) collective-permute-start(bf16[2048,128]{1,0:T(8,128)(2,1)S(1)} %get-tuple-element.41.rest_2_), channel_id=1, source_target_pairs={{0,8},{1,9},{2,10},{3,11},{4,12},{5,13},{6,14},{7,15},{8,16},{9,17... | collective-permute-start | bytes 1572872 | tf_op jit(solution)/shard_map/ppermute | solution.py:364
  22.3 0.0 collective-permute-done.2.q1.points_ref
  22.3 0.5 collective-permute-start.8
  22.8 0.1 pad_add_fusion.codes
  22.9 1.8 %sort_slots.1 = (s32[1,640]{1,0:T(1,128)S(1)}, s32[1,640]{1,0:T(1,128)S(1)}, s32[1,640]{1,0:T(1,128)S(1)}, s32[1,640]{1,0:T(1,128)S(1)}, s32[1,640]{1,0:T(1,128)S(1)}) custom-call(s32[5,128]{1,0:T(8,128)S(1)} %pad_add_fusion.codes), custom_call_target="tpu_custom_call" | custom-call | flops 500000000 | bytes 1500000 | tf_op jit(solution)/shard_map/sort_slots/pallas_call | solution.py:409
  24.7 0.0 collective-permute-done.6.q3.points_ref
  24.7 0.1 collective-permute-start
  24.7 0.0 copy-done
  24.8 2.3 %row_operands.1 = (bf16[64,128,128]{2,1,0:T(8,128)(2,1)S(1)}, f32[64,128,128]{2,1,0:T(8,128)S(1)}) custom-call(bf16[2048,128]{1,0:T(8,128)(2,1)S(1)} %copy-done, bf16[2048,128]{1,0:T(8,128)(2,1)S(1)} %collective-permute-done.2.q1.points_ref, bf16[2048,128]{1,0:T(8,128)(2,1)S(1)} %get-tuple-element.37.q2.rest_1_.points_ref, ...), custom_call_target="tpu_custom_call" | custom-call | flops 750000000 | bytes 2250000 | tf_op jit(solution)/shard_map/row_operands/pallas_call | solution.py:470
  27.1 0.0 collective-permute-done.10.rest_4_.rest_6_.rest_9_
  27.1 9.4 %tiles_0.1 = (f32[65,128,128]{2,1,0:T(8,128)S(1)}, f32[65,128,128]{2,1,0:T(8,128)S(1)}, f32[8,128]{1,0:T(8,128)S(1)}) custom-call(s32[1,640]{1,0:T(1,128)S(1)} %get-tuple-element.42.lists, bf16[64,128,128]{2,1,0:T(8,128)(2,1)S(1)} %get-tuple-element.38.rows, f32[64,128,128]{2,1,0:T(8,128)S(1)} %get-tuple-element.39.norms, bf16[2048,128]{1,0:T(8,128)(2,1)S(1)} %copy-done, ...), custom_call_target="tpu_custom_call" | custom-call | flops 1750000000 | bytes 5250000 | tf_op jit(solution)/shard_map/tiles_0/pallas_call | solution.py:430
  36.5 0.0 collective-permute-done.refs_0_.more_weights
  36.5 0.0 collective-permute-done.7.at_even.rest_2_.rest_7_
  36.5 0.0 collective-permute-done.9.second.rest_2_
  36.6 0.0 collective-permute-done.8.first.rest_1_
  36.6 0.1 third_round.1
  36.7 1.0 %collective-permute-start.17 = (bf16[2048,128]{1,0:T(8,128)(2,1)S(1)}, bf16[2048,128]{1,0:T(8,128)(2,1)S(1)}, u32[]{:S(2)}, u32[]{:S(2)}) collective-permute-start(bf16[2048,128]{1,0:T(8,128)(2,1)S(1)} %get-tuple-element.47.rest_0_), channel_id=1, source_target_pairs={{0,8},{1,9},{2,10},{3,11},{4,12},{5,13},{6,14},{7,15},{8,16},{9,17... | collective-permute-start | bytes 1572872 | tf_op jit(solution)/shard_map/ppermute | solution.py:364
  37.6 0.5 collective-permute-start.11
  38.1 1.5 %collective-permute-start.12 = (bf16[1024,128]{1,0:T(8,128)(2,1)S(1)}, bf16[1024,128]{1,0:T(8,128)(2,1)S(1)}, u32[]{:S(2)}, u32[]{:S(2)}) collective-permute-start(bf16[1024,128]{1,0:T(8,128)(2,1)S(1)} %get-tuple-element.45), channel_id=1, source_target_pairs={{0,4},{1,5},{2,6},{3,7},{4,0},{5,1},{6,2},{7,3},{8,12},{9,13},{10,... | collective-permute-start | bytes 786440 | tf_op jit(solution)/shard_map/ppermute | solution.py:364
  39.6 1.5 %collective-permute-start.15 = (bf16[1024,128]{1,0:T(8,128)(2,1)S(1)}, bf16[1024,128]{1,0:T(8,128)(2,1)S(1)}, u32[]{:S(2)}, u32[]{:S(2)}) collective-permute-start(bf16[1024,128]{1,0:T(8,128)(2,1)S(1)} %get-tuple-element.54), channel_id=1, source_target_pairs={{0,2},{1,3},{2,0},{3,1},{4,6},{5,7},{6,4},{7,5},{8,10},{9,11},{10,... | collective-permute-start | bytes 786440 | tf_op jit(solution)/shard_map/ppermute | solution.py:364
  41.1 0.5 collective-permute-start.16
  41.7 8.1 %tiles_1.1 = (f32[65,128,128]{2,1,0:T(8,128)S(1)}, f32[65,128,128]{2,1,0:T(8,128)S(1)}, f32[8,128]{1,0:T(8,128)S(1)}) custom-call(s32[1,640]{1,0:T(1,128)S(1)} %get-tuple-element.46.lists, bf16[64,128,128]{2,1,0:T(8,128)(2,1)S(1)} %get-tuple-element.38.rows, ...), custom_call_target="tpu_custom_call", output_to_operand_aliasing={{0}: (8, {}), {1}: (9, {})} | custom-call | flops 1750000000 | bytes 5250000 | tf_op jit(solution)/shard_map/tiles_1/pallas_call | solution.py:430
  49.8 0.0 collective-permute-done.11.refs_0_
  49.8 0.0 collective-permute-done.12.refs_1_
  49.8 0.4 collective-permute-start.13
  50.2 0.0 collective-permute-start.14
  50.2 0.1 collective-permute-done.15.rest_1_
  50.3 0.8 collective-permute-done.16.rest_2_
  51.1 0.9 %collective-permute-done.17.rest_4_ = bf16[2048,128]{1,0:T(8,128)(2,1)S(1)} collective-permute-done((bf16[2048,128]{1,0:T(8,128)(2,1)S(1)}, bf16[2048,128]{1,0:T(8,128)(2,1)S(1)}, u32[]{:S(2)}, u32[]{:S(2)}) %collective-permute-start.17) | collective-permute-done | bytes 524320 | tf_op jit(solution)/shard_map/ppermute | solution.py:364
  52.0 7.4 %tiles_2.1 = (f32[65,128,128]{2,1,0:T(8,128)S(1)}, f32[65,128,128]{2,1,0:T(8,128)S(1)}, f32[8,128]{1,0:T(8,128)}) custom-call(s32[1,640]{1,0:T(1,128)S(1)} %get-tuple-element.53.lists, bf16[64,128,128]{2,1,0:T(8,128)(2,1)S(1)} %get-tuple-element.38.rows, ...), custom_call_target="tpu_custom_call", output_to_operand_aliasing={{0}: (10, {}), {1}: (11, {})} | custom-call | flops 1750000000 | bytes 5250000 | tf_op jit(solution)/shard_map/tiles_2/pallas_call | solution.py:430
  59.5 0.0 collective-permute-done.13.rest_0_.rest_5_
  59.5 0.0 collective-permute-done.14.rest_1_.rest_6_
  59.5 3.0 %tiles_3.1 = (f32[65,128,128]{2,1,0:T(8,128)S(1)}, f32[65,128,128]{2,1,0:T(8,128)S(1)}, f32[8,128]{1,0:T(8,128)}) custom-call(s32[1,640]{1,0:T(1,128)S(1)} %get-tuple-element.36.lists, bf16[64,128,128]{2,1,0:T(8,128)(2,1)S(1)} %get-tuple-element.38.rows, f32[64,128,128]{2,1,0:T(8,128)S(1)} %get-tuple-element.39.norms, ...), custom_call_target="tpu_custom_call", output_to_operand_aliasing={{0}: (8, {}), {1}: (9, {})} | custom-call | flops 750000000 | bytes 2250000 | tf_op jit(solution)/shard_map/tiles_3/pallas_call | solution.py:430
  62.5 0.4 pack_core_far.1
  62.9 0.1 collective-permute-start.18
  62.9 2.6 %collective-permute-done.18.got = f32[2048,128]{1,0:T(8,128)S(1)} collective-permute-done((f32[2048,128]{1,0:T(8,128)S(1)}, f32[2048,128]{1,0:T(8,128)S(1)}, u32[]{:S(2)}, u32[]{:S(2)}) %collective-permute-start.18) | collective-permute-done | bytes 1048608 | tf_op jit(solution)/shard_map/ppermute | solution.py:364
  65.6 0.7 pack_far.1.rest_10_
  66.3 0.1 collective-permute-start.19
  66.4 7.2 %tiles_4.1 = (f32[65,128,128]{2,1,0:T(8,128)S(1)}, f32[65,128,128]{2,1,0:T(8,128)S(1)}, f32[8,128]{1,0:T(8,128)}) custom-call(s32[1,640]{1,0:T(1,128)S(1)} %get-tuple-element.63.lists, bf16[64,128,128]{2,1,0:T(8,128)(2,1)S(1)} %get-tuple-element.38.rows, ...), custom_call_target="tpu_custom_call", output_to_operand_aliasing={{0}: (14, {}), {1}: (15, {})} | custom-call | flops 12500000 | bytes 37500 | tf_op jit(solution)/shard_map/tiles_4/pallas_call | solution.py:430
  73.6 0.4 pack_core_near.1
  74.0 0.6 collective-permute-start.20
  74.6 6.1 %collective-permute-done.19.far = bf16[2112,128]{1,0:T(8,128)(2,1)S(1)} collective-permute-done((bf16[2112,128]{1,0:T(8,128)(2,1)S(1)}, bf16[2112,128]{1,0:T(8,128)(2,1)S(1)}, u32[]{:S(2)}, u32[]{:S(2)}) %collective-permute-start.19) | collective-permute-done | bytes 540704 | tf_op jit(solution)/shard_map/ppermute | solution.py:364
  80.7 0.6 from_far.1
  81.3 0.0 collective-permute-done.20.near
  81.3 1.5 %finish.1 = f32[2048,128]{1,0:T(8,128)} custom-call(f32[2048,128]{1,0:T(8,128)S(1)} %get-tuple-element.62.moved, f32[65,128,128]{2,1,0:T(8,128)S(1)} %get-tuple-element.64.pulled, f32[65,128,128]{2,1,0:T(8,128)S(1)} %get-tuple-element.65.summed, f32[2048,128]{1,0:T(8,128)S(1)} %collective-permute-done.20.near, f32[2048,128]{1,0:T(8,128)S(1)} %get-tuple-element.66.scale, ...), custom_call_target="tpu_custom_call" | custom-call | flops 250000000 | bytes 750000 | tf_op jit(solution)/shard_map/finish/pallas_call | solution.py:534
  (1 shorter events, 0.0 us)
Async XLA Ops:
  0.0 27.1 %collective-permute-start.10 = (bf16[320,128,128]{2,1,0:T(8,128)(2,1)}, bf16[320,128,128]{2,1,0:T(8,128)(2,1)}, u32[]{:S(2)}, u32[]{:S(2)}) collective-permute-start(bf16[320,128,128]{2,1,0:T(8,128)(2,1)} %bitcast.9), channel_id=1, source_target_pairs={{0,1},{1,0},{2,3},{3,2},{4,5},{5,4},{6,7},{7,6},{8,9},{9,8},{10,11... | collective-permute-start | bytes 31457288 | tf_op jit(solution)/shard_map/ppermute | solution.py:364
  0.5 17.4 %collective-permute-start.5 = (bf16[2048,128]{1,0:T(8,128)(2,1)}, bf16[2048,128]{1,0:T(8,128)(2,1)S(1)}, u32[]{:S(2)}, u32[]{:S(2)}) collective-permute-start(bf16[2048,128]{1,0:T(8,128)(2,1)} %points_ref.3), channel_id=1, source_target_pairs={{0,8},{1,9},{2,10},{3,11},{4,12},{5,13},{6,14},{7,15},{8,16},{9,17... | collective-permute-start | bytes 1572872 | tf_op jit(solution)/shard_map/ppermute | solution.py:364
  3.0 14.8 %collective-permute-start.4 = (bf16[2048,128]{1,0:T(8,128)(2,1)}, bf16[2048,128]{1,0:T(8,128)(2,1)S(1)}, u32[]{:S(2)}, u32[]{:S(2)}) collective-permute-start(bf16[2048,128]{1,0:T(8,128)(2,1)} %points_ref.3), channel_id=1, source_target_pairs={{0,2},{1,3},{2,0},{3,1},{4,6},{5,7},{6,4},{7,5},{8,10},{9,11},{10,... | collective-permute-start | bytes 1572872 | tf_op jit(solution)/shard_map/ppermute | solution.py:364
  4.5 14.0 %collective-permute-start.3 = (bf16[2048,128]{1,0:T(8,128)(2,1)}, bf16[2048,128]{1,0:T(8,128)(2,1)S(1)}, u32[]{:S(2)}, u32[]{:S(2)}) collective-permute-start(bf16[2048,128]{1,0:T(8,128)(2,1)} %points_ref.3), channel_id=1, source_target_pairs={{0,4},{1,5},{2,6},{3,7},{4,0},{5,1},{6,2},{7,3},{8,12},{9,13},{10,... | collective-permute-start | bytes 1572872 | tf_op jit(solution)/shard_map/ppermute | solution.py:364
  6.0 16.3 %collective-permute-start.2 = (bf16[2048,128]{1,0:T(8,128)(2,1)}, bf16[2048,128]{1,0:T(8,128)(2,1)S(1)}, u32[]{:S(2)}, u32[]{:S(2)}) collective-permute-start(bf16[2048,128]{1,0:T(8,128)(2,1)} %points_ref.3), channel_id=1, source_target_pairs={{0,1},{1,0},{2,3},{3,2},{4,5},{5,4},{6,7},{7,6},{8,9},{9,8},{10,11... | collective-permute-start | bytes 1572872 | tf_op jit(solution)/shard_map/ppermute | solution.py:364
  7.5 0.7 copy-start.1
  8.2 16.5 %copy-start = (bf16[2048,128]{1,0:T(8,128)(2,1)S(1)}, bf16[2048,128]{1,0:T(8,128)(2,1)}, u32[]{:S(2)}) copy-start(bf16[2048,128]{1,0:T(8,128)(2,1)} %points_ref.3) | copy-start | bytes 1572868
  18.6 6.0 %collective-permute-start.6 = (bf16[2048,128]{1,0:T(8,128)(2,1)S(1)}, bf16[2048,128]{1,0:T(8,128)(2,1)S(1)}, u32[]{:S(2)}, u32[]{:S(2)}) collective-permute-start(bf16[2048,128]{1,0:T(8,128)(2,1)S(1)} %get-tuple-element.37.q2.rest_1_.points_ref), channel_id=1, source_target_pairs={{0,1},{1,0},{2,3},{3,2},{4,5},{5,4},{6,7},{7,6},{8,9},{9,8},{10,11... | collective-permute-start | bytes 1572872 | tf_op jit(solution)/shard_map/ppermute | solution.py:364
  18.7 2.0 %collective-permute-start.1 = (s32[5,64]{1,0:T(8,128)S(1)}, s32[5,64]{1,0:T(8,128)S(1)}, u32[]{:S(2)}, u32[]{:S(2)}) collective-permute-start(s32[5,64]{1,0:T(8,128)S(1)} %fusion.1.codes), channel_id=1, source_target_pairs={{0,1},{1,0},{2,3},{3,2},{4,5},{5,4},{6,7},{7,6},{8,9},{9,8},{10,11... | collective-permute-start | bytes 3848 | tf_op jit(solution)/shard_map/ppermute | solution.py:364
  19.2 17.3 %collective-permute-start.7 = (bf16[2048,128]{1,0:T(8,128)(2,1)S(1)}, bf16[2048,128]{1,0:T(8,128)(2,1)S(1)}, u32[]{:S(2)}, u32[]{:S(2)}) collective-permute-start(bf16[2048,128]{1,0:T(8,128)(2,1)S(1)} %get-tuple-element.40), channel_id=1, source_target_pairs={{0,4},{1,5},{2,6},{3,7},{4,0},{5,1},{6,2},{7,3},{8,12},{9,13},{10,... | collective-permute-start | bytes 1572872 | tf_op jit(solution)/shard_map/ppermute | solution.py:364
  20.7 15.8 %collective-permute-start.9 = (bf16[2048,128]{1,0:T(8,128)(2,1)S(1)}, bf16[2048,128]{1,0:T(8,128)(2,1)S(1)}, u32[]{:S(2)}, u32[]{:S(2)}) collective-permute-start(bf16[2048,128]{1,0:T(8,128)(2,1)S(1)} %get-tuple-element.41.rest_2_), channel_id=1, source_target_pairs={{0,8},{1,9},{2,10},{3,11},{4,12},{5,13},{6,14},{7,15},{8,16},{9,17... | collective-permute-start | bytes 1572872 | tf_op jit(solution)/shard_map/ppermute | solution.py:364
  22.3 14.3 %collective-permute-start.8 = (bf16[2048,128]{1,0:T(8,128)(2,1)S(1)}, bf16[2048,128]{1,0:T(8,128)(2,1)S(1)}, u32[]{:S(2)}, u32[]{:S(2)}) collective-permute-start(bf16[2048,128]{1,0:T(8,128)(2,1)S(1)} %get-tuple-element.41.rest_2_), channel_id=1, source_target_pairs={{0,2},{1,3},{2,0},{3,1},{4,6},{5,7},{6,4},{7,5},{8,10},{9,11},{10,... | collective-permute-start | bytes 1572872 | tf_op jit(solution)/shard_map/ppermute | solution.py:364
  24.7 11.9 %collective-permute-start = (f32[64,128]{1,0:T(8,128)S(1)}, f32[64,128]{1,0:T(8,128)S(1)}, u32[]{:S(2)}, u32[]{:S(2)}) collective-permute-start(f32[64,128]{1,0:T(8,128)S(1)} %row_weights.1.weights), channel_id=1, source_target_pairs={{0,1},{1,0},{2,3},{3,2},{4,5},{5,4},{6,7},{7,6},{8,9},{9,8},{10,11... | collective-permute-start | bytes 98312 | tf_op jit(solution)/shard_map/ppermute | solution.py:364
  36.7 15.3 %collective-permute-start.17 = (bf16[2048,128]{1,0:T(8,128)(2,1)S(1)}, bf16[2048,128]{1,0:T(8,128)(2,1)S(1)}, u32[]{:S(2)}, u32[]{:S(2)}) collective-permute-start(bf16[2048,128]{1,0:T(8,128)(2,1)S(1)} %get-tuple-element.47.rest_0_), channel_id=1, source_target_pairs={{0,8},{1,9},{2,10},{3,11},{4,12},{5,13},{6,14},{7,15},{8,16},{9,17... | collective-permute-start | bytes 1572872 | tf_op jit(solution)/shard_map/ppermute | solution.py:364
  37.6 12.2 %collective-permute-start.11 = (bf16[1024,128]{1,0:T(8,128)(2,1)S(1)}, bf16[1024,128]{1,0:T(8,128)(2,1)S(1)}, u32[]{:S(2)}, u32[]{:S(2)}) collective-permute-start(bf16[1024,128]{1,0:T(8,128)(2,1)S(1)} %get-tuple-element.44), channel_id=1, source_target_pairs={{0,2},{1,3},{2,0},{3,1},{4,6},{5,7},{6,4},{7,5},{8,10},{9,11},{10,... | collective-permute-start | bytes 786440 | tf_op jit(solution)/shard_map/ppermute | solution.py:364
  38.1 11.7 %collective-permute-start.12 = (bf16[1024,128]{1,0:T(8,128)(2,1)S(1)}, bf16[1024,128]{1,0:T(8,128)(2,1)S(1)}, u32[]{:S(2)}, u32[]{:S(2)}) collective-permute-start(bf16[1024,128]{1,0:T(8,128)(2,1)S(1)} %get-tuple-element.45), channel_id=1, source_target_pairs={{0,4},{1,5},{2,6},{3,7},{4,0},{5,1},{6,2},{7,3},{8,12},{9,13},{10,... | collective-permute-start | bytes 786440 | tf_op jit(solution)/shard_map/ppermute | solution.py:364
  39.6 10.7 %collective-permute-start.15 = (bf16[1024,128]{1,0:T(8,128)(2,1)S(1)}, bf16[1024,128]{1,0:T(8,128)(2,1)S(1)}, u32[]{:S(2)}, u32[]{:S(2)}) collective-permute-start(bf16[1024,128]{1,0:T(8,128)(2,1)S(1)} %get-tuple-element.54), channel_id=1, source_target_pairs={{0,2},{1,3},{2,0},{3,1},{4,6},{5,7},{6,4},{7,5},{8,10},{9,11},{10,... | collective-permute-start | bytes 786440 | tf_op jit(solution)/shard_map/ppermute | solution.py:364
  41.1 9.9 %collective-permute-start.16 = (bf16[1024,128]{1,0:T(8,128)(2,1)S(1)}, bf16[1024,128]{1,0:T(8,128)(2,1)S(1)}, u32[]{:S(2)}, u32[]{:S(2)}) collective-permute-start(bf16[1024,128]{1,0:T(8,128)(2,1)S(1)} %get-tuple-element.55), channel_id=1, source_target_pairs={{0,4},{1,5},{2,6},{3,7},{4,0},{5,1},{6,2},{7,3},{8,12},{9,13},{10,... | collective-permute-start | bytes 786440 | tf_op jit(solution)/shard_map/ppermute | solution.py:364
  49.8 9.6 %collective-permute-start.13 = (bf16[1024,128]{1,0:T(8,128)(2,1)S(1)}, bf16[1024,128]{1,0:T(8,128)(2,1)S(1)}, u32[]{:S(2)}, u32[]{:S(2)}) collective-permute-start(bf16[1024,128]{1,0:T(8,128)(2,1)S(1)} %get-tuple-element.51.rest_0_), channel_id=1, source_target_pairs={{0,4},{1,5},{2,6},{3,7},{4,0},{5,1},{6,2},{7,3},{8,12},{9,13},{10,... | collective-permute-start | bytes 786440 | tf_op jit(solution)/shard_map/ppermute | solution.py:364
  50.2 9.2 %collective-permute-start.14 = (bf16[1024,128]{1,0:T(8,128)(2,1)S(1)}, bf16[1024,128]{1,0:T(8,128)(2,1)S(1)}, u32[]{:S(2)}, u32[]{:S(2)}) collective-permute-start(bf16[1024,128]{1,0:T(8,128)(2,1)S(1)} %get-tuple-element.52.rest_3_), channel_id=1, source_target_pairs={{0,8},{1,9},{2,10},{3,11},{4,12},{5,13},{6,14},{7,15},{8,16},{9,17... | collective-permute-start | bytes 786440 | tf_op jit(solution)/shard_map/ppermute | solution.py:364
  62.9 2.7 %collective-permute-start.18 = (f32[2048,128]{1,0:T(8,128)S(1)}, f32[2048,128]{1,0:T(8,128)S(1)}, u32[]{:S(2)}, u32[]{:S(2)}) collective-permute-start(f32[2048,128]{1,0:T(8,128)S(1)} %pack_core_far.1), channel_id=1, source_target_pairs={{0,1},{1,0},{2,3},{3,2},{4,5},{5,4},{6,7},{7,6},{8,9},{9,8},{10,11... | collective-permute-start | bytes 3145736 | tf_op jit(solution)/shard_map/ppermute | solution.py:364
  66.3 14.4 %collective-permute-start.19 = (bf16[2112,128]{1,0:T(8,128)(2,1)S(1)}, bf16[2112,128]{1,0:T(8,128)(2,1)S(1)}, u32[]{:S(2)}, u32[]{:S(2)}) collective-permute-start(bf16[2112,128]{1,0:T(8,128)(2,1)S(1)} %pack_far.1.rest_10_), channel_id=1, source_target_pairs={{0,2},{1,3},{2,0},{3,1},{4,6},{5,7},{6,4},{7,5},{8,10},{9,11},{10,... | collective-permute-start | bytes 1622024 | tf_op jit(solution)/shard_map/ppermute | solution.py:364
  74.0 7.3 %collective-permute-start.20 = (f32[2048,128]{1,0:T(8,128)S(1)}, f32[2048,128]{1,0:T(8,128)S(1)}, u32[]{:S(2)}, u32[]{:S(2)}) collective-permute-start(f32[2048,128]{1,0:T(8,128)S(1)} %pack_core_near.1), channel_id=1, source_target_pairs={{0,1},{1,0},{2,3},{3,2},{4,5},{5,4},{6,7},{7,6},{8,9},{9,8},{10,11... | collective-permute-start | bytes 3145736 | tf_op jit(solution)/shard_map/ppermute | solution.py:364

commit v2 on v1

--- a/solution.py
+++ b/solution.py
@@ -49,10 +49,15 @@
     return jnp.sum(jnp.where(diagonal(row.shape[1]), row, 0.0), axis=1, keepdims=True)
 
 
-def lists_kernel(stride, per_quarter, codes, *outs):
+def lists_kernel(stride, per_quarter, offsets, own, other, *outs):
     rep, even = place_of_device(stride)
     core, mine = rep & 1, lax.shift_right_arithmetic(rep, 1)
-    offsets, width = codes.shape
+    width, tail = own.shape[1], pl.ds(other.shape[0] - own.shape[0], own.shape[0])
+    slots = width // 2
+    own, other = own[...].astype(jnp.float32), other[tail, :].astype(jnp.float32)
+    first = lanes_of(own.shape) < slots
+    all_rows = jnp.where(first, own, pltpu.roll(other, slots, axis=1)).astype(jnp.int32)
+    all_columns = jnp.where(first, pltpu.roll(own, slots, axis=1), other).astype(jnp.int32)
     room = outs[0].shape[1] - 128
     lanes = lanes_of((1, width))
     later = lax.broadcasted_iota(jnp.int32, (width, width), 0) <= lanes_of((width, width))
@@ -65,12 +70,11 @@
             here = [(m, *pair) for m, pair in enumerate(arrays) if offset in (pair[0] // 2, pair[1] // 2)]
             if not here:
                 continue
-            code = codes[offset : offset + 1, :]
-            row, col = lax.shift_right_arithmetic(code, 8), code & 255
+            row, col = all_rows[offset : offset + 1, :], all_columns[offset : offset + 1, :]
             quarter, row_half = jnp.zeros_like(col), jnp.where(row >= 2 * per_quarter, 1, 0)
             for edge in range(1, 4):
                 quarter += jnp.where(col >= edge * per_quarter, 1, 0)
-            live = code >= 0
+            live = row >= 0
             if side_of_rows is not ALL:
                 live = live & ((row_half != mine) if side_of_rows else (row_half == mine))
             match = jnp.zeros((1, width), jnp.float32)
@@ -94,7 +98,6 @@
             )
         listed = listed.astype(jnp.int32)
         lane, row, column, offset = listed[0:1], listed[8:9], listed[16:17], listed[24:25]
-        slots = width // 2
         tile = offset * slots + lane + jnp.where(lane >= slots, (offsets - 1) * slots, 0)
         outs[stage][:, :room] = tile * 65536 + row * 256 + column
         outs[stage][:, room:] = jnp.broadcast_to(before.astype(jnp.int32), (1, 128))
@@ -130,14 +133,15 @@
         lax.fori_loop(0, blocks // 8, close, 0)
 
 
-def rows_kernel(q0, q1, q2, q3, out, norms):
+def rows_kernel(count, own, partner, out, norms):
     side = out.shape[1]
-    count = q0.shape[0] // side
-    for index, quarter in enumerate((q0, q1, q2, q3)):
+    for index in range(4):
         holder = jnp.bitwise_xor(lax.axis_index("rep"), index)
-
-        def visit(block, carry, quarter=quarter, holder=holder):
-            points = quarter[pl.ds(pl.multiple_of(block * side, side), side), :].astype(jnp.float32)
+        source, first = (own, partner)[index % 2], index // 2 * count
+
+        def visit(block, carry, source=source, first=first, holder=holder):
+            rows = pl.ds(pl.multiple_of((first + block) * side, side), side)
+            points = source[rows, :].astype(jnp.float32)
             out[holder * count + block] = (-2.0 * points).astype(jnp.bfloat16)
             norm = jnp.sum(points * points, axis=1, keepdims=True) + 1.0
             norms[holder * count + block] = jnp.broadcast_to(norm, (side, side))
@@ -236,19 +240,24 @@
     pass
 
 
-def second_round_kernel(stride, weights, early, near, far, *refs):
-    near_out, far_out, across = refs[-3:]
+def second_round_kernel(weights, early, blocks_of, own, near, far, message, far_out):
+    count = near.shape[0]
+    message[:count, :] = own[...]
+    message[count : 2 * count, :] = near[...]
+    message[2 * count :, :] = blocks_of[...]
+    far_out[...] = far[...]
+
+
+def choose_kernel(stride, at_even, at_odd, out):
     even = place_of_device(stride)[1]
-    near_out[...] = near[...]
-    far_out[...] = far[...]
 
     @pl.when(even)
     def _():
-        across[...] = near[...]
+        out[...] = at_even[pl.ds(out.shape[0], out.shape[0]), :]
 
     @pl.when(jnp.logical_not(even))
     def _():
-        across[...] = far[...]
+        out[...] = at_odd[...]
 
 
 def third_round_kernel(stride, at_even, at_odd, first, second, *refs):
@@ -278,7 +287,8 @@
     base = jnp.bitwise_xor(lax.axis_index("rep"), flip) * count
     for block in range(count):
         rows = slice(block * side, (block + 1) * side)
-        out[rows, :] = drift(pulled, summed, base + block, points_ref[rows, :].astype(jnp.float32))
+        points = points_ref[(flip // 2 * count + block) * side : (flip // 2 * count + block + 1) * side, :]
+        out[rows, :] = drift(pulled, summed, base + block, points.astype(jnp.float32))
 
 
 def pack_far_kernel(pulled, summed, norms, weights, more_weights, got, points_ref, out):
@@ -382,7 +392,8 @@
     codes = tile_blocks[0, :, :, 0] * 256 + tile_blocks[0, :, :, 1]
     alive = jnp.arange(slots, dtype=jnp.int32)[None, :] < tile_count[0][:, None]
     codes = jnp.where(alive, codes, -1)
-    other_codes = along_core(codes)
+    blocks_of = jnp.concatenate([jnp.where(alive, tile_blocks[0, :, :, 0], -1), tile_blocks[0, :, :, 1]], axis=1)
+    blocks_of = jnp.pad(blocks_of.astype(coords.dtype), ((0, 16 - offsets), (0, 0)))
     other_targets = along_core(targets)
 
     def gated(values, *tokens):
@@ -406,14 +417,39 @@
         out_specs=vmem,
         scratch_shapes=[VMEM((blocks + 1, side, side), jnp.float32)],
     )(codes, tile_count[0], pltpu.with_memory_space_constraint(dissim[0], HBM))
+    p20 = along_z(coords)
+    p01 = along_y(coords)
+    a10 = along_x(coords)
+    whole = jax.ShapeDtypeStruct((own_rows, width), coords.dtype)
+    message, p20 = kernel_call(
+        second_round_kernel,
+        "second_round",
+        0.5,
+        out_shape=(jax.ShapeDtypeStruct((2 * own_rows + 16, width), coords.dtype), whole),
+        in_specs=[anywhere] * 2 + [vmem] * 4,
+        out_specs=(vmem,) * 2,
+    )(weights, a10, blocks_of, coords, p01, p20)
+    p40 = along_z(p20)
+    p21 = along_y(p20)
+    across = kernel_call(
+        functools.partial(choose_kernel, stride),
+        "choose",
+        0.5,
+        out_shape=whole,
+        in_specs=[vmem] * 2,
+        out_specs=vmem,
+    )(message, p20)
+    r10 = along_x(across)
+    partner = along_core(message)
+    more_weights = along_core(weights)
     lists = kernel_call(
-        functools.partial(lists_kernel, stride, count),
+        functools.partial(lists_kernel, stride, count, offsets),
         "sort_slots",
         2,
         out_shape=(jax.ShapeDtypeStruct((1, 2 * slots * (offsets - 1) + 128), jnp.int32),) * len(STAGES),
-        in_specs=[vmem],
+        in_specs=[vmem] * 2,
         out_specs=(vmem,) * len(STAGES),
-    )(jnp.concatenate([codes, other_codes], axis=1))
+    )(blocks_of, partner)
     def tiles(stage, sums, *places, tokens=()):
         first = sums is None
         points, layout, at = [], [], 0
@@ -448,33 +484,14 @@
             ],
         )(lists[stage], rows, norms, *points, targets, other_targets, *tokens, *([] if first else sums))
         return out[:2], out[2]
-
-    p20 = along_z(coords)
-    p01 = along_y(coords)
-    a10 = along_x(coords)
-    near_rows = along_core(coords)
-    whole = jax.ShapeDtypeStruct((own_rows, width), coords.dtype)
-    p01, p20, across = kernel_call(
-        functools.partial(second_round_kernel, stride),
-        "second_round",
-        0.5,
-        out_shape=(whole,) * 3,
-        in_specs=[anywhere] * 2 + [vmem] * 2,
-        out_specs=(vmem,) * 3,
-    )(weights, a10, p01, p20)
-    p40 = along_z(p20)
-    p21 = along_y(p20)
-    r10 = along_x(across)
-    far_rows = along_core(p01)
-    more_weights = along_core(weights)
     rows, norms = kernel_call(
-        rows_kernel,
+        functools.partial(rows_kernel, count),
         "row_operands",
         3,
         out_shape=(VMEM((blocks, side, side), jnp.bfloat16), VMEM((blocks, side, side), jnp.float32)),
-        in_specs=[vmem] * 4,
+        in_specs=[vmem] * 2,
         out_specs=(vmem, vmem),
-    )(coords, near_rows, p01, far_rows)
+    )(message, partner)
     rows = pltpu.with_memory_space_constraint(rows, VMEM)
     norms = pltpu.with_memory_space_constraint(norms, VMEM)
 
@@ -510,7 +527,7 @@
         )(*sums, points)
 
     sums = [pltpu.with_memory_space_constraint(value, VMEM) for value in sums]
-    got_far = along_core(pack_core(3, "pack_core_far", far_rows))
+    got_far = along_core(pack_core(3, "pack_core_far", partner))
     to_far = kernel_call(
         pack_far_kernel,
         "pack_far",
@@ -522,7 +539,7 @@
     far = along_y(to_far)
     sums, token = tiles(4, sums, (p41a, p41b), (t21a, t21b), (p30,), last, tokens=(to_far,))
     sums = [pltpu.with_memory_space_constraint(value, VMEM) for value in sums]
-    got_near = along_core(pack_core(1, "pack_core_near", near_rows))
+    got_near = along_core(pack_core(1, "pack_core_near", partner))
     moved, scale = kernel_call(
         from_far_kernel,
         "from_far",

time: 83.8 us -> 83.2 us (level)
  Pallas kernels: 52.1 us -> 46.7 us
  waiting for transfers between devices: 11.7 us -> 14.3 us
  starting transfers between devices: 16.4 us -> 18.5 us
    pallas_call x5, Pallas kernels: 35.2 us -> 29.7 us  [tiles(): kernel_call(functools.partial(stage_kernel, first, layout, stride, len(to...]
    ppermute x21 -> x19, waiting for transfers between devices: 11.7 us -> 14.3 us  [sent(): return lax.ppermute(value, ('col', 'rep'), pairs)]
    ppermute x21 -> x19, starting transfers between devices: 16.4 us -> 18.5 us  [sent(): return lax.ppermute(value, ('col', 'rep'), pairs)]
    pallas_call x3 -> x4, Pallas kernels: 4.19 us -> 4.31 us  [the longest x1 2.31 us: per_device(): kernel_call(functools.partial(rows_kernel, count), 'row_operands', 3, out...]
  transfers between devices with their start and end apart: 21 -> 19, of which waited for: 7 -> 8; matrix products, arithmetic and copies ran while one was open for 2% -> 2% of each run, Pallas kernels for 56% -> 50%
where the time goes in v2:
time: 83.2 us; the launch traced here: 81.9 us
  Pallas kernels  46.7 us (56%)
  starting transfers between devices  18.5 us (22%)
  waiting for transfers between devices  14.3 us (17%)
  local copies, waits for them, and re-layouts  1.43 us (2%)
    pallas_call x5, Pallas kernels, tiles(): kernel_call(functools.partial(stage_kernel, first, layout, stride, len(to...  29.7 us
    ppermute x19, starting transfers between devices, sent(): return lax.ppermute(value, ('col', 'rep'), pairs)  18.5 us
    ppermute x19, waiting for transfers between devices, sent(): return lax.ppermute(value, ('col', 'rep'), pairs)  14.3 us
    pallas_call x1, Pallas kernels, per_device(): kernel_call(weights_kernel, 'row_weights', 9, out_shape=jax.ShapeDtypeStr...  9.1 us
    pallas_call x1, Pallas kernels, per_device(): kernel_call(functools.partial(rows_kernel, count), 'row_operands', 3, out...  2.31 us
    pallas_call x1, Pallas kernels, per_device(): kernel_call(functools.partial(lists_kernel, stride, count, offsets), 'sor...  1.84 us
  transfers between devices with their start and end apart: 19, of which 8 were waited for; matrix products, arithmetic and copies ran while one was open for 2% of the time, Pallas kernels for 50%

profile of v2, /device:TPU:0, one launch (start us, length us, event | category | flops | bytes accessed | tf_op | source)
XLA Modules:
  0.0 81.9 jit_solution(18106840323851092301)
XLA Ops:
  0.0 0.5 collective-permute-start.8
  0.5 2.6 %collective-permute-start.3 = (bf16[2048,128]{1,0:T(8,128)(2,1)}, bf16[2048,128]{1,0:T(8,128)(2,1)S(1)}, u32[]{:S(2)}, u32[]{:S(2)}) collective-permute-start(bf16[2048,128]{1,0:T(8,128)(2,1)} %points_ref.3), channel_id=1, source_target_pairs={{0,8},{1,9},{2,10},{3,11},{4,12},{5,13},{6,14},{7,15},{8,16},{9,17... | collective-permute-start | bytes 1572872 | tf_op jit(solution)/shard_map/ppermute | solution.py:374
  3.0 1.5 %collective-permute-start.2 = (bf16[2048,128]{1,0:T(8,128)(2,1)}, bf16[2048,128]{1,0:T(8,128)(2,1)S(1)}, u32[]{:S(2)}, u32[]{:S(2)}) collective-permute-start(bf16[2048,128]{1,0:T(8,128)(2,1)} %points_ref.3), channel_id=1, source_target_pairs={{0,2},{1,3},{2,0},{3,1},{4,6},{5,7},{6,4},{7,5},{8,10},{9,11},{10,... | collective-permute-start | bytes 1572872 | tf_op jit(solution)/shard_map/ppermute | solution.py:374
  4.5 1.5 %collective-permute-start.1 = (bf16[2048,128]{1,0:T(8,128)(2,1)}, bf16[2048,128]{1,0:T(8,128)(2,1)S(1)}, u32[]{:S(2)}, u32[]{:S(2)}) collective-permute-start(bf16[2048,128]{1,0:T(8,128)(2,1)} %points_ref.3), channel_id=1, source_target_pairs={{0,4},{1,5},{2,6},{3,7},{4,0},{5,1},{6,2},{7,3},{8,12},{9,13},{10,... | collective-permute-start | bytes 1572872 | tf_op jit(solution)/shard_map/ppermute | solution.py:374
  6.0 0.8 fusion.9
  6.8 0.7 fusion.8
  7.5 0.1 fusion.2.blocks_of.own
  7.6 0.0 copy-start.1
  7.6 0.7 copy-done.1
  8.3 0.0 copy-start
  8.3 9.1 %row_weights.1.weights = f32[64,128]{1,0:T(8,128)S(1)} custom-call(s32[5,64]{1,0:T(8,128)S(1)} %get-tuple-element.68.codes, s32[5]{0:T(128)S(1)} %bitcast.22, bf16[5,64,128,128]{3,2,1,0:T(8,128)(2,1)} %bitcast.24), custom_call_target="tpu_custom_call" | custom-call | flops 2249999872 | bytes 6750000 | tf_op jit(solution)/shard_map/row_weights/pallas_call | solution.py:410
  17.4 0.5 collective-permute-done.3.far
  17.9 0.0 collective-permute-done.2.near.rest_1_.points_ref
  17.9 0.7 collective-permute-done.1.early.at_odd
  18.5 0.0 copy-done
  18.5 0.1 second_round.1
  18.6 0.1 collective-permute-start.4
  18.7 0.1 choose.1
  18.8 1.6 %collective-permute-start.5 = (bf16[2048,128]{1,0:T(8,128)(2,1)S(1)}, bf16[2048,128]{1,0:T(8,128)(2,1)S(1)}, u32[]{:S(2)}, u32[]{:S(2)}) collective-permute-start(bf16[2048,128]{1,0:T(8,128)(2,1)S(1)} %choose.1), channel_id=1, source_target_pairs={{0,4},{1,5},{2,6},{3,7},{4,0},{5,1},{6,2},{7,3},{8,12},{9,13},{10,... | collective-permute-start | bytes 1572872 | tf_op jit(solution)/shard_map/ppermute | solution.py:374
  20.3 1.6 %collective-permute-start.7 = (bf16[2048,128]{1,0:T(8,128)(2,1)S(1)}, bf16[2048,128]{1,0:T(8,128)(2,1)S(1)}, u32[]{:S(2)}, u32[]{:S(2)}) collective-permute-start(bf16[2048,128]{1,0:T(8,128)(2,1)S(1)} %get-tuple-element.39.at_odd.rest_2_), channel_id=1, source_target_pairs={{0,8},{1,9},{2,10},{3,11},{4,12},{5,13},{6,14},{7,15},{8,16},{9,17... | collective-permute-start | bytes 1572872 | tf_op jit(solution)/shard_map/ppermute | solution.py:374
  21.9 0.5 collective-permute-start.6
  22.4 0.0 collective-permute-done.4.other.partner.points_ref
  22.4 0.0 collective-permute-start
  22.4 1.8 %sort_slots.1 = (s32[1,640]{1,0:T(1,128)S(1)}, s32[1,640]{1,0:T(1,128)S(1)}, s32[1,640]{1,0:T(1,128)S(1)}, s32[1,640]{1,0:T(1,128)S(1)}, s32[1,640]{1,0:T(1,128)S(1)}) custom-call(bf16[16,128]{1,0:T(8,128)(2,1)S(1)} %fusion.2.blocks_of.own, bf16[4112,128]{1,0:T(8,128)(2,1)S(1)} %collective-permute-done.4.other.partner.points_ref), custom_call_target="tpu_custom_call" | custom-call | flops 500000000 | bytes 1500000 | tf_op jit(solution)/shard_map/sort_slots/pallas_call | solution.py:445
  24.3 2.3 %row_operands.1 = (bf16[64,128,128]{2,1,0:T(8,128)(2,1)S(1)}, f32[64,128,128]{2,1,0:T(8,128)S(1)}) custom-call(bf16[4112,128]{1,0:T(8,128)(2,1)S(1)} %get-tuple-element.35.own.at_even, bf16[4112,128]{1,0:T(8,128)(2,1)S(1)} %collective-permute-done.4.other.partner.points_ref), custom_call_target="tpu_custom_call" | custom-call | flops 750000000 | bytes 2250000 | tf_op jit(solution)/shard_map/row_operands/pallas_call | solution.py:487
  26.6 0.0 collective-permute-done.8.rest_4_.rest_6_.rest_9_
  26.6 8.2 %tiles_0.1 = (f32[65,128,128]{2,1,0:T(8,128)S(1)}, f32[65,128,128]{2,1,0:T(8,128)S(1)}, f32[8,128]{1,0:T(8,128)S(1)}) custom-call(s32[1,640]{1,0:T(1,128)S(1)} %get-tuple-element.40.lists, bf16[64,128,128]{2,1,0:T(8,128)(2,1)S(1)} %get-tuple-element.37.rows, f32[64,128,128]{2,1,0:T(8,128)S(1)} %get-tuple-element.38.norms, bf16[2048,128]{1,0:T(8,128)(2,1)S(1)} %copy-done, ...), custom_call_target="tpu_custom_call" | custom-call | flops 1750000000 | bytes 5250000 | tf_op jit(solution)/shard_map/tiles_0/pallas_call | solution.py:466
  34.8 0.0 collective-permute-done.refs_0_.more_weights
  34.8 0.0 collective-permute-done.5.at_even.rest_2_.rest_7_
  34.8 1.3 %collective-permute-done.7.second.rest_2_ = bf16[2048,128]{1,0:T(8,128)(2,1)S(1)} collective-permute-done((bf16[2048,128]{1,0:T(8,128)(2,1)S(1)}, bf16[2048,128]{1,0:T(8,128)(2,1)S(1)}, u32[]{:S(2)}, u32[]{:S(2)}) %collective-permute-start.7) | collective-permute-done | bytes 524320 | tf_op jit(solution)/shard_map/ppermute | solution.py:374
  36.2 0.0 collective-permute-done.6.first.rest_1_
  36.2 0.1 third_round.1
  36.3 1.1 %collective-permute-start.15 = (bf16[2048,128]{1,0:T(8,128)(2,1)S(1)}, bf16[2048,128]{1,0:T(8,128)(2,1)S(1)}, u32[]{:S(2)}, u32[]{:S(2)}) collective-permute-start(bf16[2048,128]{1,0:T(8,128)(2,1)S(1)} %get-tuple-element.45.rest_0_), channel_id=1, source_target_pairs={{0,8},{1,9},{2,10},{3,11},{4,12},{5,13},{6,14},{7,15},{8,16},{9,17... | collective-permute-start | bytes 1572872 | tf_op jit(solution)/shard_map/ppermute | solution.py:374
  37.4 0.5 collective-permute-start.9
  37.9 0.5 collective-permute-start.10
  38.4 1.5 %collective-permute-start.13 = (bf16[1024,128]{1,0:T(8,128)(2,1)S(1)}, bf16[1024,128]{1,0:T(8,128)(2,1)S(1)}, u32[]{:S(2)}, u32[]{:S(2)}) collective-permute-start(bf16[1024,128]{1,0:T(8,128)(2,1)S(1)} %get-tuple-element.52), channel_id=1, source_target_pairs={{0,2},{1,3},{2,0},{3,1},{4,6},{5,7},{6,4},{7,5},{8,10},{9,11},{10,... | collective-permute-start | bytes 786440 | tf_op jit(solution)/shard_map/ppermute | solution.py:374
  40.0 1.5 %collective-permute-start.14 = (bf16[1024,128]{1,0:T(8,128)(2,1)S(1)}, bf16[1024,128]{1,0:T(8,128)(2,1)S(1)}, u32[]{:S(2)}, u32[]{:S(2)}) collective-permute-start(bf16[1024,128]{1,0:T(8,128)(2,1)S(1)} %get-tuple-element.53), channel_id=1, source_target_pairs={{0,4},{1,5},{2,6},{3,7},{4,0},{5,1},{6,2},{7,3},{8,12},{9,13},{10,... | collective-permute-start | bytes 786440 | tf_op jit(solution)/shard_map/ppermute | solution.py:374
  41.5 6.1 %tiles_1.1 = (f32[65,128,128]{2,1,0:T(8,128)S(1)}, f32[65,128,128]{2,1,0:T(8,128)S(1)}, f32[8,128]{1,0:T(8,128)S(1)}) custom-call(s32[1,640]{1,0:T(1,128)S(1)} %get-tuple-element.44.lists, bf16[64,128,128]{2,1,0:T(8,128)(2,1)S(1)} %get-tuple-element.37.rows, ...), custom_call_target="tpu_custom_call", output_to_operand_aliasing={{0}: (8, {}), {1}: (9, {})} | custom-call | flops 1750000000 | bytes 5250000 | tf_op jit(solution)/shard_map/tiles_1/pallas_call | solution.py:466
  47.5 0.0 collective-permute-done.9.refs_0_
  47.5 0.0 collective-permute-done.10.refs_1_
  47.6 2.2 %collective-permute-start.11 = (bf16[1024,128]{1,0:T(8,128)(2,1)S(1)}, bf16[1024,128]{1,0:T(8,128)(2,1)S(1)}, u32[]{:S(2)}, u32[]{:S(2)}) collective-permute-start(bf16[1024,128]{1,0:T(8,128)(2,1)S(1)} %get-tuple-element.49.rest_0_), channel_id=1, source_target_pairs={{0,4},{1,5},{2,6},{3,7},{4,0},{5,1},{6,2},{7,3},{8,12},{9,13},{10,... | collective-permute-start | bytes 786440 | tf_op jit(solution)/shard_map/ppermute | solution.py:374
  49.8 0.0 collective-permute-start.12
  49.8 0.2 collective-permute-done.13.rest_1_
  50.0 1.7 %collective-permute-done.14.rest_2_ = bf16[1024,128]{1,0:T(8,128)(2,1)S(1)} collective-permute-done((bf16[1024,128]{1,0:T(8,128)(2,1)S(1)}, bf16[1024,128]{1,0:T(8,128)(2,1)S(1)}, u32[]{:S(2)}, u32[]{:S(2)}) %collective-permute-start.14) | collective-permute-done | bytes 262176 | tf_op jit(solution)/shard_map/ppermute | solution.py:374
  51.7 0.8 collective-permute-done.15.rest_4_
  52.5 6.0 %tiles_2.1 = (f32[65,128,128]{2,1,0:T(8,128)S(1)}, f32[65,128,128]{2,1,0:T(8,128)S(1)}, f32[8,128]{1,0:T(8,128)}) custom-call(s32[1,640]{1,0:T(1,128)S(1)} %get-tuple-element.51.lists, bf16[64,128,128]{2,1,0:T(8,128)(2,1)S(1)} %get-tuple-element.37.rows, ...), custom_call_target="tpu_custom_call", output_to_operand_aliasing={{0}: (10, {}), {1}: (11, {})} | custom-call | flops 1750000000 | bytes 5250000 | tf_op jit(solution)/shard_map/tiles_2/pallas_call | solution.py:466
  58.6 0.0 collective-permute-done.11.rest_0_.rest_5_
  58.6 0.0 collective-permute-done.12.rest_1_.rest_6_
  58.6 3.1 %tiles_3.1 = (f32[65,128,128]{2,1,0:T(8,128)S(1)}, f32[65,128,128]{2,1,0:T(8,128)S(1)}, f32[8,128]{1,0:T(8,128)}) custom-call(s32[1,640]{1,0:T(1,128)S(1)} %get-tuple-element.36.lists, bf16[64,128,128]{2,1,0:T(8,128)(2,1)S(1)} %get-tuple-element.37.rows, f32[64,128,128]{2,1,0:T(8,128)S(1)} %get-tuple-element.38.norms, ...), custom_call_target="tpu_custom_call", output_to_operand_aliasing={{0}: (8, {}), {1}: (9, {})} | custom-call | flops 750000000 | bytes 2250000 | tf_op jit(solution)/shard_map/tiles_3/pallas_call | solution.py:466
  61.6 0.4 pack_core_far.1
  62.0 0.1 collective-permute-start.16
  62.1 2.6 %collective-permute-done.16.got = f32[2048,128]{1,0:T(8,128)S(1)} collective-permute-done((f32[2048,128]{1,0:T(8,128)S(1)}, f32[2048,128]{1,0:T(8,128)S(1)}, u32[]{:S(2)}, u32[]{:S(2)}) %collective-permute-start.16) | collective-permute-done | bytes 1048608 | tf_op jit(solution)/shard_map/ppermute | solution.py:374
  64.7 0.7 pack_far.1.rest_10_
  65.5 1.2 %collective-permute-start.17 = (bf16[2112,128]{1,0:T(8,128)(2,1)S(1)}, bf16[2112,128]{1,0:T(8,128)(2,1)S(1)}, u32[]{:S(2)}, u32[]{:S(2)}) collective-permute-start(bf16[2112,128]{1,0:T(8,128)(2,1)S(1)} %pack_far.1.rest_10_), channel_id=1, source_target_pairs={{0,2},{1,3},{2,0},{3,1},{4,6},{5,7},{6,4},{7,5},{8,10},{9,11},{10,... | collective-permute-start | bytes 1622024 | tf_op jit(solution)/shard_map/ppermute | solution.py:374
  66.6 6.3 %tiles_4.1 = (f32[65,128,128]{2,1,0:T(8,128)S(1)}, f32[65,128,128]{2,1,0:T(8,128)S(1)}, f32[8,128]{1,0:T(8,128)}) custom-call(s32[1,640]{1,0:T(1,128)S(1)} %get-tuple-element.61.lists, bf16[64,128,128]{2,1,0:T(8,128)(2,1)S(1)} %get-tuple-element.37.rows, ...), custom_call_target="tpu_custom_call", output_to_operand_aliasing={{0}: (14, {}), {1}: (15, {})} | custom-call | flops 12500000 | bytes 37500 | tf_op jit(solution)/shard_map/tiles_4/pallas_call | solution.py:466
  72.9 0.4 pack_core_near.1
  73.3 0.1 collective-permute-start.18
  73.4 6.5 %collective-permute-done.17.far = bf16[2112,128]{1,0:T(8,128)(2,1)S(1)} collective-permute-done((bf16[2112,128]{1,0:T(8,128)(2,1)S(1)}, bf16[2112,128]{1,0:T(8,128)(2,1)S(1)}, u32[]{:S(2)}, u32[]{:S(2)}) %collective-permute-start.17) | collective-permute-done | bytes 540704 | tf_op jit(solution)/shard_map/ppermute | solution.py:374
  79.8 0.6 from_far.1
  80.5 0.0 collective-permute-done.18.near
  80.5 1.4 %finish.1 = f32[2048,128]{1,0:T(8,128)} custom-call(f32[2048,128]{1,0:T(8,128)S(1)} %get-tuple-element.60.moved, f32[65,128,128]{2,1,0:T(8,128)S(1)} %get-tuple-element.62.pulled, f32[65,128,128]{2,1,0:T(8,128)S(1)} %get-tuple-element.63.summed, f32[2048,128]{1,0:T(8,128)S(1)} %collective-permute-done.18.near, f32[2048,128]{1,0:T(8,128)S(1)} %get-tuple-element.64.scale, ...), custom_call_target="tpu_custom_call" | custom-call | flops 250000000 | bytes 750000 | tf_op jit(solution)/shard_map/finish/pallas_call | solution.py:551
  (2 shorter events, 0.0 us)
Async XLA Ops:
  0.0 26.6 %collective-permute-start.8 = (bf16[320,128,128]{2,1,0:T(8,128)(2,1)}, bf16[320,128,128]{2,1,0:T(8,128)(2,1)}, u32[]{:S(2)}, u32[]{:S(2)}) collective-permute-start(bf16[320,128,128]{2,1,0:T(8,128)(2,1)} %bitcast.23), channel_id=1, source_target_pairs={{0,1},{1,0},{2,3},{3,2},{4,5},{5,4},{6,7},{7,6},{8,9},{9,8},{10,11... | collective-permute-start | bytes 31457288 | tf_op jit(solution)/shard_map/ppermute | solution.py:374
  0.5 17.4 %collective-permute-start.3 = (bf16[2048,128]{1,0:T(8,128)(2,1)}, bf16[2048,128]{1,0:T(8,128)(2,1)S(1)}, u32[]{:S(2)}, u32[]{:S(2)}) collective-permute-start(bf16[2048,128]{1,0:T(8,128)(2,1)} %points_ref.3), channel_id=1, source_target_pairs={{0,8},{1,9},{2,10},{3,11},{4,12},{5,13},{6,14},{7,15},{8,16},{9,17... | collective-permute-start | bytes 1572872 | tf_op jit(solution)/shard_map/ppermute | solution.py:374
  3.0 14.8 %collective-permute-start.2 = (bf16[2048,128]{1,0:T(8,128)(2,1)}, bf16[2048,128]{1,0:T(8,128)(2,1)S(1)}, u32[]{:S(2)}, u32[]{:S(2)}) collective-permute-start(bf16[2048,128]{1,0:T(8,128)(2,1)} %points_ref.3), channel_id=1, source_target_pairs={{0,2},{1,3},{2,0},{3,1},{4,6},{5,7},{6,4},{7,5},{8,10},{9,11},{10,... | collective-permute-start | bytes 1572872 | tf_op jit(solution)/shard_map/ppermute | solution.py:374
  4.5 14.0 %collective-permute-start.1 = (bf16[2048,128]{1,0:T(8,128)(2,1)}, bf16[2048,128]{1,0:T(8,128)(2,1)S(1)}, u32[]{:S(2)}, u32[]{:S(2)}) collective-permute-start(bf16[2048,128]{1,0:T(8,128)(2,1)} %points_ref.3), channel_id=1, source_target_pairs={{0,4},{1,5},{2,6},{3,7},{4,0},{5,1},{6,2},{7,3},{8,12},{9,13},{10,... | collective-permute-start | bytes 1572872 | tf_op jit(solution)/shard_map/ppermute | solution.py:374
  7.6 0.7 copy-start.1
  8.3 10.3 %copy-start = (bf16[2048,128]{1,0:T(8,128)(2,1)S(1)}, bf16[2048,128]{1,0:T(8,128)(2,1)}, u32[]{:S(2)}) copy-start(bf16[2048,128]{1,0:T(8,128)(2,1)} %points_ref.3) | copy-start | bytes 1572868
  18.6 3.8 %collective-permute-start.4 = (bf16[4112,128]{1,0:T(8,128)(2,1)S(1)}, bf16[4112,128]{1,0:T(8,128)(2,1)S(1)}, u32[]{:S(2)}, u32[]{:S(2)}) collective-permute-start(bf16[4112,128]{1,0:T(8,128)(2,1)S(1)} %get-tuple-element.35.own.at_even), channel_id=1, source_target_pairs={{0,1},{1,0},{2,3},{3,2},{4,5},{5,4},{6,7},{7,6},{8,9},{9,8},{10,11... | collective-permute-start | bytes 3158024 | tf_op jit(solution)/shard_map/ppermute | solution.py:374
  18.8 16.1 %collective-permute-start.5 = (bf16[2048,128]{1,0:T(8,128)(2,1)S(1)}, bf16[2048,128]{1,0:T(8,128)(2,1)S(1)}, u32[]{:S(2)}, u32[]{:S(2)}) collective-permute-start(bf16[2048,128]{1,0:T(8,128)(2,1)S(1)} %choose.1), channel_id=1, source_target_pairs={{0,4},{1,5},{2,6},{3,7},{4,0},{5,1},{6,2},{7,3},{8,12},{9,13},{10,... | collective-permute-start | bytes 1572872 | tf_op jit(solution)/shard_map/ppermute | solution.py:374
  20.3 15.8 %collective-permute-start.7 = (bf16[2048,128]{1,0:T(8,128)(2,1)S(1)}, bf16[2048,128]{1,0:T(8,128)(2,1)S(1)}, u32[]{:S(2)}, u32[]{:S(2)}) collective-permute-start(bf16[2048,128]{1,0:T(8,128)(2,1)S(1)} %get-tuple-element.39.at_odd.rest_2_), channel_id=1, source_target_pairs={{0,8},{1,9},{2,10},{3,11},{4,12},{5,13},{6,14},{7,15},{8,16},{9,17... | collective-permute-start | bytes 1572872 | tf_op jit(solution)/shard_map/ppermute | solution.py:374
  21.9 14.2 %collective-permute-start.6 = (bf16[2048,128]{1,0:T(8,128)(2,1)S(1)}, bf16[2048,128]{1,0:T(8,128)(2,1)S(1)}, u32[]{:S(2)}, u32[]{:S(2)}) collective-permute-start(bf16[2048,128]{1,0:T(8,128)(2,1)S(1)} %get-tuple-element.39.at_odd.rest_2_), channel_id=1, source_target_pairs={{0,2},{1,3},{2,0},{3,1},{4,6},{5,7},{6,4},{7,5},{8,10},{9,11},{10,... | collective-permute-start | bytes 1572872 | tf_op jit(solution)/shard_map/ppermute | solution.py:374
  22.4 12.4 %collective-permute-start = (f32[64,128]{1,0:T(8,128)S(1)}, f32[64,128]{1,0:T(8,128)S(1)}, u32[]{:S(2)}, u32[]{:S(2)}) collective-permute-start(f32[64,128]{1,0:T(8,128)S(1)} %row_weights.1.weights), channel_id=1, source_target_pairs={{0,1},{1,0},{2,3},{3,2},{4,5},{5,4},{6,7},{7,6},{8,9},{9,8},{10,11... | collective-permute-start | bytes 98312 | tf_op jit(solution)/shard_map/ppermute | solution.py:374
  36.3 16.2 %collective-permute-start.15 = (bf16[2048,128]{1,0:T(8,128)(2,1)S(1)}, bf16[2048,128]{1,0:T(8,128)(2,1)S(1)}, u32[]{:S(2)}, u32[]{:S(2)}) collective-permute-start(bf16[2048,128]{1,0:T(8,128)(2,1)S(1)} %get-tuple-element.45.rest_0_), channel_id=1, source_target_pairs={{0,8},{1,9},{2,10},{3,11},{4,12},{5,13},{6,14},{7,15},{8,16},{9,17... | collective-permute-start | bytes 1572872 | tf_op jit(solution)/shard_map/ppermute | solution.py:374
  37.4 10.1 %collective-permute-start.9 = (bf16[1024,128]{1,0:T(8,128)(2,1)S(1)}, bf16[1024,128]{1,0:T(8,128)(2,1)S(1)}, u32[]{:S(2)}, u32[]{:S(2)}) collective-permute-start(bf16[1024,128]{1,0:T(8,128)(2,1)S(1)} %get-tuple-element.42), channel_id=1, source_target_pairs={{0,2},{1,3},{2,0},{3,1},{4,6},{5,7},{6,4},{7,5},{8,10},{9,11},{10,... | collective-permute-start | bytes 786440 | tf_op jit(solution)/shard_map/ppermute | solution.py:374
  37.9 9.6 %collective-permute-start.10 = (bf16[1024,128]{1,0:T(8,128)(2,1)S(1)}, bf16[1024,128]{1,0:T(8,128)(2,1)S(1)}, u32[]{:S(2)}, u32[]{:S(2)}) collective-permute-start(bf16[1024,128]{1,0:T(8,128)(2,1)S(1)} %get-tuple-element.43), channel_id=1, source_target_pairs={{0,4},{1,5},{2,6},{3,7},{4,0},{5,1},{6,2},{7,3},{8,12},{9,13},{10,... | collective-permute-start | bytes 786440 | tf_op jit(solution)/shard_map/ppermute | solution.py:374
  38.4 11.6 %collective-permute-start.13 = (bf16[1024,128]{1,0:T(8,128)(2,1)S(1)}, bf16[1024,128]{1,0:T(8,128)(2,1)S(1)}, u32[]{:S(2)}, u32[]{:S(2)}) collective-permute-start(bf16[1024,128]{1,0:T(8,128)(2,1)S(1)} %get-tuple-element.52), channel_id=1, source_target_pairs={{0,2},{1,3},{2,0},{3,1},{4,6},{5,7},{6,4},{7,5},{8,10},{9,11},{10,... | collective-permute-start | bytes 786440 | tf_op jit(solution)/shard_map/ppermute | solution.py:374
  40.0 11.7 %collective-permute-start.14 = (bf16[1024,128]{1,0:T(8,128)(2,1)S(1)}, bf16[1024,128]{1,0:T(8,128)(2,1)S(1)}, u32[]{:S(2)}, u32[]{:S(2)}) collective-permute-start(bf16[1024,128]{1,0:T(8,128)(2,1)S(1)} %get-tuple-element.53), channel_id=1, source_target_pairs={{0,4},{1,5},{2,6},{3,7},{4,0},{5,1},{6,2},{7,3},{8,12},{9,13},{10,... | collective-permute-start | bytes 786440 | tf_op jit(solution)/shard_map/ppermute | solution.py:374
  47.6 11.0 %collective-permute-start.11 = (bf16[1024,128]{1,0:T(8,128)(2,1)S(1)}, bf16[1024,128]{1,0:T(8,128)(2,1)S(1)}, u32[]{:S(2)}, u32[]{:S(2)}) collective-permute-start(bf16[1024,128]{1,0:T(8,128)(2,1)S(1)} %get-tuple-element.49.rest_0_), channel_id=1, source_target_pairs={{0,4},{1,5},{2,6},{3,7},{4,0},{5,1},{6,2},{7,3},{8,12},{9,13},{10,... | collective-permute-start | bytes 786440 | tf_op jit(solution)/shard_map/ppermute | solution.py:374
  49.8 8.8 %collective-permute-start.12 = (bf16[1024,128]{1,0:T(8,128)(2,1)S(1)}, bf16[1024,128]{1,0:T(8,128)(2,1)S(1)}, u32[]{:S(2)}, u32[]{:S(2)}) collective-permute-start(bf16[1024,128]{1,0:T(8,128)(2,1)S(1)} %get-tuple-element.50.rest_3_), channel_id=1, source_target_pairs={{0,8},{1,9},{2,10},{3,11},{4,12},{5,13},{6,14},{7,15},{8,16},{9,17... | collective-permute-start | bytes 786440 | tf_op jit(solution)/shard_map/ppermute | solution.py:374
  62.0 2.7 %collective-permute-start.16 = (f32[2048,128]{1,0:T(8,128)S(1)}, f32[2048,128]{1,0:T(8,128)S(1)}, u32[]{:S(2)}, u32[]{:S(2)}) collective-permute-start(f32[2048,128]{1,0:T(8,128)S(1)} %pack_core_far.1), channel_id=1, source_target_pairs={{0,1},{1,0},{2,3},{3,2},{4,5},{5,4},{6,7},{7,6},{8,9},{9,8},{10,11... | collective-permute-start | bytes 3145736 | tf_op jit(solution)/shard_map/ppermute | solution.py:374
  65.5 14.4 %collective-permute-start.17 = (bf16[2112,128]{1,0:T(8,128)(2,1)S(1)}, bf16[2112,128]{1,0:T(8,128)(2,1)S(1)}, u32[]{:S(2)}, u32[]{:S(2)}) collective-permute-start(bf16[2112,128]{1,0:T(8,128)(2,1)S(1)} %pack_far.1.rest_10_), channel_id=1, source_target_pairs={{0,2},{1,3},{2,0},{3,1},{4,6},{5,7},{6,4},{7,5},{8,10},{9,11},{10,... | collective-permute-start | bytes 1622024 | tf_op jit(solution)/shard_map/ppermute | solution.py:374
  73.3 7.2 %collective-permute-start.18 = (f32[2048,128]{1,0:T(8,128)S(1)}, f32[2048,128]{1,0:T(8,128)S(1)}, u32[]{:S(2)}, u32[]{:S(2)}) collective-permute-start(f32[2048,128]{1,0:T(8,128)S(1)} %pack_core_near.1), channel_id=1, source_target_pairs={{0,1},{1,0},{2,3},{3,2},{4,5},{5,4},{6,7},{7,6},{8,9},{9,8},{10,11... | collective-permute-start | bytes 3145736 | tf_op jit(solution)/shard_map/ppermute | solution.py:374
